TPU v7x, 256 devices: a whole 4x4x8 slice. The times are simulated.
256 devices in a mesh: rows: 32 (over z, y), cols: 8 (over x, core).
Axes of the slice: x: 4, y: 4, z: 8, core: 2. Of those that a mesh axis runs over, the one named last changes fastest.
Arguments:
- source_cells: bfloat16 [64, 262144], P(None, 'rows'), may hold values from -21 to 21
- target_cells: bfloat16 [64, 262144], P(None, 'cols'), may hold values from -21 to 21
- source_logmass: float32 [262144], P('rows'), may hold values from -3 to 3
- target_logmass: float32 [262144], P('cols'), may hold values from -3 to 3
- neighbours: int32 [2048, 16], P('rows'), may hold values from 0 to 2047, as said below
Outputs:
- source_potential: float32 [262144], P('rows')
- target_potential: float32 [262144], P('cols')
Inputs may be any that keep to these rules, and one draw needn't show every extreme that they name: `neighbours`: each row names 16 distinct target blocks and every target block is named by some row. No row names more than 4 blocks of one range c * 256 to (c + 1) * 256 - 1, and in every draw some rows name exactly 4 of one range; how many entries of a row fall in one range depends only on the row's rows index.
All inputs are finite; a program needn't handle non-finite values.
Results may differ from a plain program's by a relative error of at most 0.0003.
Values sent between devices are 32-bit elements; how exact they have to be, the bound alone decides.
A program may use at most 128 MiB of HBM per device.

v0:
```python
import math

import jax
import jax.numpy as jnp
from jax import lax
from jax.sharding import PartitionSpec as P

BLOCK = 128
LIST = 16
ITERS = 3


EPS = 0.05
NEG = -1e30


def on_device(source_cells, target_cells, source_logmass, target_logmass, neighbours):
    features = source_cells.shape[0]
    src_blocks = neighbours.shape[0]
    tgt_blocks = target_cells.shape[1] // BLOCK
    n_cols = lax.axis_size("cols")
    slots = 2 * LIST // n_cols
    col_index = lax.axis_index("cols")
    owned = neighbours // tgt_blocks == col_index
    sort_keys = jnp.where(owned, 0, LIST) + jnp.arange(LIST, dtype=jnp.int32)[None, :]
    ordering = jnp.argsort(sort_keys, axis=1)[:, :slots]
    picked = jnp.take_along_axis(neighbours, ordering, axis=1)
    usable = jnp.take_along_axis(owned, ordering, axis=1)
    slot_ids = jnp.where(usable, picked - col_index * tgt_blocks, 0)
    src_three = source_cells.reshape(features, src_blocks, BLOCK)
    tgt_three = target_cells.reshape(features, tgt_blocks, BLOCK)
    src_squares = jnp.sum(jnp.square(src_three.astype(jnp.float32)), axis=0)
    tgt_squares = jnp.sum(jnp.square(tgt_three.astype(jnp.float32)), axis=0)
    group_size = math.gcd(src_blocks, 8)
    group_count = src_blocks // group_size
    grouped_cells = jnp.moveaxis(src_three.reshape(features, group_count, group_size, BLOCK), 1, 0)
    grouped_squares = src_squares.reshape(group_count, group_size, BLOCK)
    grouped_ids = slot_ids.reshape(group_count, group_size, slots)
    grouped_usable = usable.reshape(group_count, group_size, slots)
    src_mass = source_logmass.reshape(src_blocks, BLOCK)
    tgt_mass = target_logmass.reshape(tgt_blocks, BLOCK)
    flat_ids = slot_ids.reshape(-1)

    def tile_costs(cells_in, squares, ids_in):
        gathered = tgt_three[:, ids_in, :]
        crossed = jnp.einsum(
            "dgi,dgsj->gisj", cells_in, gathered, preferred_element_type=jnp.float32
        )
        return (
            squares[:, :, None, None] + tgt_squares[ids_in][:, None, :, :] - 2.0 * crossed
        ) / features

    target_pot = jnp.zeros((tgt_blocks, BLOCK), jnp.float32)
    source_pot = jnp.zeros((src_blocks, BLOCK), jnp.float32)
    for step in range(ITERS):

        def source_side(args):
            cells_in, squares, ids_in, usable_in = args
            costs = tile_costs(cells_in, squares, ids_in)
            mask = usable_in[:, None, :, None]
            scores = jnp.where(mask, (target_pot[ids_in][:, None, :, :] - costs) / EPS, NEG)
            highest = jnp.max(scores, axis=(2, 3))
            totals = jnp.sum(
                jnp.where(mask, jnp.exp(scores - highest[:, :, None, None]), 0.0), axis=(2, 3)
            )
            return (highest, totals)

        highest, totals = lax.map(
            source_side, (grouped_cells, grouped_squares, grouped_ids, grouped_usable)
        )
        highest = highest.reshape(src_blocks, BLOCK)
        totals = totals.reshape(src_blocks, BLOCK)
        peak_all = lax.pmax(highest, "cols")
        totals = lax.psum(totals * jnp.exp(highest - peak_all), "cols")
        highest = peak_all
        source_pot = EPS * (src_mass - (highest + jnp.log(totals)))
        grouped_pot = source_pot.reshape(group_count, group_size, BLOCK)

        def target_side(args):
            cells_in, squares, ids_in, usable_in, potential = args
            costs = tile_costs(cells_in, squares, ids_in)
            scores = (potential[:, :, None, None] - costs) / EPS
            peaks = jnp.max(scores, axis=1)
            sums = jnp.sum(jnp.exp(scores - peaks[:, None, :, :]), axis=1)
            keep = usable_in[:, :, None]
            return (jnp.where(keep, peaks, NEG), jnp.where(keep, sums, 0.0))

        peaks, sums = lax.map(
            target_side, (grouped_cells, grouped_squares, grouped_ids, grouped_usable, grouped_pot)
        )
        peaks = peaks.reshape(-1, BLOCK)
        sums = sums.reshape(-1, BLOCK)
        block_peak = jnp.full((tgt_blocks, BLOCK), NEG, jnp.float32).at[flat_ids].max(peaks)
        scaled = sums * jnp.exp(peaks - block_peak[flat_ids])
        summed = jax.ops.segment_sum(scaled, flat_ids, num_segments=tgt_blocks)
        peak_rows = lax.pmax(block_peak, "rows")
        total_rows = lax.psum(summed * jnp.exp(block_peak - peak_rows), "rows")
        target_pot = EPS * (tgt_mass - (peak_rows + jnp.log(total_rows)))
    return (source_pot.reshape(-1), target_pot.reshape(-1))


def solution(mesh):
    placed = (P(None, "rows"), P(None, "cols"), P("rows"), P("cols"), P("rows", None))
    return jax.shard_map(
        on_device, mesh=mesh, in_specs=placed, out_specs=(P("rows"), P("cols")), check_vma=False
    )
```

profile of v0, /device:TPU:1, one launch (start us, length us, event | category | flops | bytes accessed | tf_op | source)
XLA Modules:
  0.0 1323.4 jit_solution(1178361214784331147)
XLA Ops:
  7.2 5.5 copy_bitcast_fusion
  21.1 56.9 %while.72 = (s32[]{:T(128)}, f32[8,8,128]{2,1,0:T(8,128)S(1)}, f32[8,8,128]{2,1,0:T(8,128)S(1)}, pred[8,8,4]{1,2,0:T(4,128)(4,1)S(1)}, s32[8,8,4]{1,2,0:T(4,128)...) while((s32[]{:T(128)}, f32[8,8,128]{2,1,0:T(8,128)S(1)}, ...), condition=%wide.region_6.7_spmd, body=%wide.region_3.6_spmd.sunk | while | flops 72875104 | bytes 6175269 | solution.py:68
  78.0 23.6 %pmax.42 = f32[64,128]{1,0:T(8,128)S(1)} all-reduce(f32[64,128]{1,0:T(8,128)S(1)} %bitcast.383), channel_id=1, replica_groups=mesh['rows'=32,'cols'=8] {'cols'}, use_global_device_ids=true, to_apply=%region_7.8 | all-reduce | flops 8192 | bytes 65536 | tf_op jit(solution)/shard_map/pmax | solution.py:73
  101.6 23.6 %psum.42 = f32[64,128]{1,0:T(8,128)S(1)} all-reduce(f32[64,128]{1,0:T(8,128)S(1)} %bitcast_multiply_fusion.2), channel_id=1, replica_groups=mesh['rows'=32,'cols'=8] {'cols'}, use_global_device_ids=true, to_apply=%region_8.9 | all-reduce | flops 8192 | bytes 65536 | tf_op jit(solution)/shard_map/psum | solution.py:74
  125.3 42.0 %while.73 = (s32[]{:T(128)}, f32[8,8,4,128]{3,2,1,0:T(4,128)S(1)}, f32[8,8,4,128]{3,2,1,0:T(4,128)S(1)}, pred[8,8,4]{1,2,0:T(4,128)(4,1)S(1)}, f32[8,8,128]{2,1,...) while((s32[]{:T(128)}, f32[8,8,4,128]{3,2,1,0:T(4,128)S(1)}, ...), condition=%wide.region_12.13_spmd, body=%wide.region_9.12_spmd.sunk | while | flops 71828576 | bytes 6093185 | solution.py:88
  167.5 3.0 scatter_custom_fusion
  170.6 12.4 scatter_custom_fusion.1
  183.0 127.5 %all-reduce.7.cloned.1.call-done = f32[256,128]{1,0:T(8,128)} async-done(((f32[256,128]{1,0:T(8,128)}), f32[256,128]{1,0:T(8,128)}) %all-reduce.7.cloned.1.call-update) | async-done | bytes 131088 | tf_op jit(solution)/shard_map/pmax | solution.py:96
  312.3 141.9 %all-reduce.9.cloned.1.call-done = f32[256,128]{1,0:T(8,128)} async-done(((f32[256,128]{1,0:T(8,128)}), f32[256,128]{1,0:T(8,128)}) %all-reduce.9.cloned.1.call-update) | async-done | bytes 131088 | tf_op jit(solution)/shard_map/psum | solution.py:97
  455.2 56.7 %while.74 = (s32[]{:T(128)}, f32[8,8,128]{2,1,0:T(8,128)S(1)}, f32[8,8,128]{2,1,0:T(8,128)S(1)}, pred[8,8,4]{1,2,0:T(4,128)(4,1)S(1)}, s32[8,8,4]{1,2,0:T(4,128)...) while((s32[]{:T(128)}, f32[8,8,128]{2,1,0:T(8,128)S(1)}, ...), condition=%wide.region_20.21_spmd, body=%wide.region_17.20_spmd.sunk | while | flops 72875104 | bytes 6044193 | solution.py:68
  511.9 24.5 %pmax.44 = f32[64,128]{1,0:T(8,128)S(1)} all-reduce(f32[64,128]{1,0:T(8,128)S(1)} %bitcast.384), channel_id=1, replica_groups=mesh['rows'=32,'cols'=8] {'cols'}, use_global_device_ids=true, to_apply=%region_21.22 | all-reduce | flops 8192 | bytes 65536 | tf_op jit(solution)/shard_map/pmax | solution.py:73
  536.4 23.8 %psum.44 = f32[64,128]{1,0:T(8,128)S(1)} all-reduce(f32[64,128]{1,0:T(8,128)S(1)} %bitcast_multiply_fusion.1), channel_id=1, replica_groups=mesh['rows'=32,'cols'=8] {'cols'}, use_global_device_ids=true, to_apply=%region_22.23 | all-reduce | flops 8192 | bytes 65536 | tf_op jit(solution)/shard_map/psum | solution.py:74
  560.3 42.0 %while.75 = (s32[]{:T(128)}, f32[8,8,4,128]{3,2,1,0:T(4,128)S(1)}, f32[8,8,4,128]{3,2,1,0:T(4,128)S(1)}, pred[8,8,4]{1,2,0:T(4,128)(4,1)S(1)}, f32[8,8,128]{2,1,...) while((s32[]{:T(128)}, f32[8,8,4,128]{3,2,1,0:T(4,128)S(1)}, ...), condition=%wide.region_26.27_spmd, body=%wide.region_23.26_spmd.sunk | while | flops 71828576 | bytes 6093185 | solution.py:88
  602.2 3.0 scatter_custom_fusion.2
  605.3 12.4 scatter_custom_fusion.3
  617.7 123.2 %all-reduce.11.cloned.1.call-done = f32[256,128]{1,0:T(8,128)} async-done(((f32[256,128]{1,0:T(8,128)}), f32[256,128]{1,0:T(8,128)}) %all-reduce.11.cloned.1.call-update) | async-done | bytes 131088 | tf_op jit(solution)/shard_map/pmax | solution.py:96
  742.6 141.7 %all-reduce.13.cloned.1.call-done = f32[256,128]{1,0:T(8,128)} async-done(((f32[256,128]{1,0:T(8,128)}), f32[256,128]{1,0:T(8,128)}) %all-reduce.13.cloned.1.call-update) | async-done | bytes 131088 | tf_op jit(solution)/shard_map/psum | solution.py:97
  885.4 56.7 %while.76 = (s32[]{:T(128)}, f32[8,8,128]{2,1,0:T(8,128)S(1)}, f32[8,8,128]{2,1,0:T(8,128)S(1)}, pred[8,8,4]{1,2,0:T(4,128)(4,1)S(1)}, s32[8,8,4]{1,2,0:T(4,128)...) while((s32[]{:T(128)}, f32[8,8,128]{2,1,0:T(8,128)S(1)}, ...), condition=%wide.region_34.35_spmd, body=%wide.region_31.34_spmd.sunk | while | flops 72875104 | bytes 6044193 | solution.py:68
  942.1 24.5 %pmax.46 = f32[64,128]{1,0:T(8,128)S(1)} all-reduce(f32[64,128]{1,0:T(8,128)S(1)} %bitcast.385), channel_id=1, replica_groups=mesh['rows'=32,'cols'=8] {'cols'}, use_global_device_ids=true, to_apply=%region_35.36 | all-reduce | flops 8192 | bytes 65536 | tf_op jit(solution)/shard_map/pmax | solution.py:73
  966.6 23.6 %psum.46 = f32[64,128]{1,0:T(8,128)S(1)} all-reduce(f32[64,128]{1,0:T(8,128)S(1)} %bitcast_multiply_fusion), channel_id=1, replica_groups=mesh['rows'=32,'cols'=8] {'cols'}, use_global_device_ids=true, to_apply=%region_36.37 | all-reduce | flops 8192 | bytes 65536 | tf_op jit(solution)/shard_map/psum | solution.py:74
  990.9 42.0 %while.77 = (s32[]{:T(128)}, f32[8,8,4,128]{3,2,1,0:T(4,128)S(1)}, f32[8,8,4,128]{3,2,1,0:T(4,128)S(1)}, pred[8,8,4]{1,2,0:T(4,128)(4,1)S(1)}, f32[8,8,128]{2,1,...) while((s32[]{:T(128)}, f32[8,8,4,128]{3,2,1,0:T(4,128)S(1)}, ...), condition=%wide.region_40.41_spmd, body=%wide.region_37.40_spmd.sunk | while | flops 71828576 | bytes 6093185 | solution.py:88
  1035.9 12.4 scatter_custom_fusion.5
  1048.3 123.2 %all-reduce.15.cloned.1.call-done = f32[256,128]{1,0:T(8,128)} async-done(((f32[256,128]{1,0:T(8,128)}), f32[256,128]{1,0:T(8,128)}) %all-reduce.15.cloned.1.call-update) | async-done | bytes 131088 | tf_op jit(solution)/shard_map/pmax | solution.py:96
  1173.2 141.8 %all-reduce.17.cloned.1.call-done = f32[256,128]{1,0:T(8,128)} async-done(((f32[256,128]{1,0:T(8,128)}), f32[256,128]{1,0:T(8,128)}) %all-reduce.17.cloned.1.call-update) | async-done | bytes 131088 | tf_op jit(solution)/shard_map/psum | solution.py:97
  (682 shorter events, 314.7 us)
Async XLA Ops:
  7.2 303.4 %all-reduce.7.cloned.1.call-start = ((), (), s32[]{:S(2)}) async-start(), calls=%async_computation | async-start | bytes 262144 | tf_op jit(solution)/shard_map/pmax | solution.py:96
  7.2 5.5 copy-start.1
  12.7 1.0 copy-start
  16.7 3.1 copy-start.2
  21.0 104.2 %copy-start.4 = (f32[8192]{0:T(1024)S(1)}, f32[8192]{0:T(1024)}, u32[]{:S(2)}) copy-start(f32[8192]{0:T(1024)} %param.19) | copy-start | bytes 98308
  125.3 328.9 %copy-start.3 = (f32[32768]{0:T(1024)S(1)}, f32[32768]{0:T(1024)}, u32[]{:S(2)}) copy-start(f32[32768]{0:T(1024)} %param.20) | copy-start | bytes 393220
  170.5 283.7 %all-reduce.9.cloned.1.call-start = ((), (), s32[]{:S(2)}) async-start(), calls=%async_computation.1 | async-start | bytes 262144 | tf_op jit(solution)/shard_map/psum | solution.py:97
  312.2 428.7 %all-reduce.11.cloned.1.call-start = ((), (), s32[]{:S(2)}) async-start(), calls=%async_computation.2 | async-start | bytes 262144 | tf_op jit(solution)/shard_map/pmax | solution.py:96
  605.2 279.1 %all-reduce.13.cloned.1.call-start = ((), (), s32[]{:S(2)}) async-start(), calls=%async_computation.3 | async-start | bytes 262144 | tf_op jit(solution)/shard_map/psum | solution.py:97
  742.6 428.9 %all-reduce.15.cloned.1.call-start = ((), (), s32[]{:S(2)}) async-start(), calls=%async_computation.4 | async-start | bytes 262144 | tf_op jit(solution)/shard_map/pmax | solution.py:96
  1035.8 279.1 %all-reduce.17.cloned.1.call-start = ((), (), s32[]{:S(2)}) async-start(), calls=%async_computation.5 | async-start | bytes 262144 | tf_op jit(solution)/shard_map/psum | solution.py:97
Sparse Core Ops, SparseCore 0:
  170.6 139.9 all-reduce.6
  315.0 139.1 all-reduce.8
  605.4 135.4 all-reduce.10
  745.2 139.1 all-reduce.12
  1036.0 135.4 all-reduce.14
  1175.8 139.1 all-reduce.16
where the time goes:
time: 1330 us; the launch traced here: 1320 us
  waiting for transfers between devices  799 us (60%)
  local copies, waits for them, and re-layouts  203 us (15%)
  blocking collectives  144 us (11%)
  other arithmetic  81.6 us (6%)
  matrix products  78.5 us (6%)
  between operations  14.5 us (1%)
    psum x3, waiting for transfers between devices, on_device(): total_rows = lax.psum(summed * jnp.exp(block_peak - peak_rows), 'rows')  425 us
    pmax x3, waiting for transfers between devices, on_device(): peak_rows = lax.pmax(block_peak, 'rows')  374 us
    gather x48, local copies, waits for them, and re-layouts, tile_costs(): gathered = tgt_three[:, ids_in, :]  136 us
    dot_general x48, matrix products, tile_costs(): jnp.einsum('dgi,dgsj->gisj', cells_in, gathered, preferred_element_type=j...  78.5 us
    pmax x3, blocking collectives, on_device(): peak_all = lax.pmax(highest, 'cols')  72.6 us
    psum x3, blocking collectives, on_device(): totals = lax.psum(totals * jnp.exp(highest - peak_all), 'cols')  71 us
    scatter-add x3, other arithmetic, on_device(): summed = jax.ops.segment_sum(scaled, flat_ids, num_segments=tgt_blocks)  37.1 us
    gather x48, local copies, waits for them, and re-layouts, tile_costs(): tgt_squares[ids_in][:, None, :, :]  27.5 us
  transfers between devices with their start and end apart: 6, of which 6 were waited for; matrix products, arithmetic and copies ran while one was open for 3% of the time, Pallas kernels for 0%

commit v1 on v0

v1 whole, which is shorter than its diff:
```python
import functools
import math

import jax
import jax.numpy as jnp
from jax import lax
from jax.experimental import pallas as pl
from jax.experimental.pallas import tpu as pltpu
from jax.sharding import PartitionSpec as P

BLOCK = 128
LIST = 16
ITERS = 3
SLOTS = 4
EPS = 0.05
NEG = -1e30
LOG2E = math.log2(math.e)
UNIT = EPS / LOG2E
CHUNKS = 4
SCAN = (1, 2, 4, 8, 16, 32)
MESH = pl.DeviceIdType.MESH


def log2(v):
    return jnp.log(v) * LOG2E


def kernel(
    n_rows, n_cols, remote,
    ids_ref, trow_ref, tcol_ref, x_ref, y_ref, a_ref, b_ref,
    f_ref, g_ref,
    cells_y, tile, gam, sqx, sqy, hits, first, last, masks, part, src, trg, landing, own,
    y_sem, src_send, src_recv, trg_send, trg_recv, own_send, own_recv,
):
    dim = x_ref.shape[0]
    kappa = 2.0 * LOG2E / (dim * EPS)
    sb, tb = x_ref.shape[1] // BLOCK, y_ref.shape[1] // BLOCK
    pairs = sb * SLOTS
    share = tb // n_rows
    step = sb // CHUNKS
    if remote:
        me_r, me_c = lax.axis_index("rows"), lax.axis_index("cols")
        barrier = pltpu.get_barrier_semaphore()

        @pl.loop(1, n_rows)
        def _(d):
            pl.semaphore_signal(
                barrier, inc=1, device_id={"rows": lax.rem(me_r + d, n_rows)}, device_id_type=MESH
            )

        @pl.loop(1, n_cols)
        def _(d):
            pl.semaphore_signal(
                barrier, inc=1, device_id={"cols": lax.rem(me_c + d, n_cols)}, device_id_type=MESH
            )
    else:
        me_r = me_c = 0

    @pl.loop(0, tb, unroll=8)
    def _(t):
        pltpu.make_async_copy(
            y_ref.at[:, pl.ds(pl.multiple_of(t * BLOCK, BLOCK), BLOCK)], cells_y.at[t], y_sem
        ).start()

    cells_y[tb] = jnp.zeros((dim, BLOCK), jnp.bfloat16)
    pltpu.make_async_copy(cells_y.at[pl.ds(0, tb)], cells_y.at[pl.ds(0, tb)], y_sem).wait()

    @pl.loop(0, tb, unroll=8)
    def _(t):
        cells = cells_y[t].astype(jnp.float32)
        squares = jnp.sum(cells * cells, axis=0, keepdims=True) * (0.5 * kappa)
        sqy[pl.ds(t, 1), :] = squares
        gam[pl.ds(t, 1), :] = -squares

    gam[pl.ds(tb, 8), :] = jnp.full((8, BLOCK), NEG, jnp.float32)

    @pl.loop(0, sb, unroll=8)
    def _(b):
        cells = x_ref[:, pl.ds(pl.multiple_of(b * BLOCK, BLOCK), BLOCK)].astype(jnp.float32)
        sqx[pl.ds(b, 1), :] = jnp.sum(cells * cells, axis=0, keepdims=True) * (0.5 * kappa)

    tr, tc = trow_ref[...], tcol_ref[...]
    ip = lax.broadcasted_iota(jnp.int32, (pairs, pairs), 0)
    iq = lax.broadcasted_iota(jnp.int32, (pairs, pairs), 1)
    before = (tc < tr) | ((tc == tr) & (ip < iq))
    place = jnp.sum(jnp.where(before, 1.0, 0.0), axis=0, keepdims=True)
    put = place == ip.astype(jnp.float32)
    first[...] = jnp.where(put, 1.0, 0.0).astype(jnp.bfloat16)
    trf = tr.astype(jnp.float32)
    ordered = jnp.sum(jnp.where(put, trf, 0.0), axis=1, keepdims=True)
    it_ = lax.broadcasted_iota(jnp.int32, (tb, pairs), 0)
    iu = lax.broadcasted_iota(jnp.int32, (tb, pairs), 1)
    upto = jnp.sum(jnp.where(tr <= it_, 1.0, 0.0), axis=1, keepdims=True)
    count = jnp.sum(jnp.where(tr == it_, 1.0, 0.0), axis=1, keepdims=True)
    at = jnp.where(count > 0.0, upto - 1.0, -1.0)
    last[...] = jnp.where(iu.astype(jnp.float32) == at, 1.0, 0.0).astype(jnp.bfloat16)
    hits[...] = jnp.broadcast_to(jnp.where(count > 0.0, 0.0, NEG), (tb, BLOCK))
    wide = jnp.broadcast_to(ordered, (pairs, BLOCK))
    rows = lax.broadcasted_iota(jnp.int32, (pairs, BLOCK), 0)
    for k, d in enumerate(SCAN):
        same = (wide == pltpu.roll(wide, d, 0)) & (rows >= d)
        masks[k] = jnp.where(same, 0.0, NEG)

    @pl.loop(0, sb)
    def _(b):
        cells = x_ref[:, pl.ds(pl.multiple_of(b * BLOCK, BLOCK), BLOCK)]
        listed = []
        for s in range(SLOTS):
            listed.append(cells_y[ids_ref[b * SLOTS + s]])
        crossed = lax.dot_general(
            cells, jnp.concatenate(listed, axis=1), (((0,), (0,)), ((), ())),
            preferred_element_type=jnp.float32,
        )
        tile[b] = crossed * kappa

    if remote:
        pl.semaphore_wait(barrier, n_rows + n_cols - 2)

    lanes = lax.broadcasted_iota(jnp.int32, (BLOCK, BLOCK), 1)

    def pick(onehot, v):
        high = v.astype(jnp.bfloat16)
        rest = v - high.astype(jnp.float32)
        middle = rest.astype(jnp.bfloat16)
        low = (rest - middle.astype(jnp.float32)).astype(jnp.bfloat16)
        out = jnp.dot(
            onehot, jnp.concatenate([high, middle, low], axis=1), preferred_element_type=jnp.float32
        )
        return (out[:, :BLOCK] + out[:, BLOCK : 2 * BLOCK]) + out[:, 2 * BLOCK :]

    @pl.loop(0, ITERS)
    def _(it):
        for q in range(CHUNKS):

            def source_block(k, acc):
                b = q * step + k
                scores = []
                for s in range(SLOTS):
                    row = gam[ids_ref[b * SLOTS + s]][None, :]
                    scores.append(tile[b, :, s * BLOCK : (s + 1) * BLOCK] + row)
                peak = functools.reduce(jnp.maximum, scores)
                peak = jnp.max(peak, axis=1, keepdims=True)
                total = functools.reduce(jnp.add, [jnp.exp2(v - peak) for v in scores])
                total = jnp.sum(total, axis=1, keepdims=True)
                return jnp.where(lanes == k, peak + log2(total), acc)

            acc = lax.fori_loop(
                0, step, source_block, jnp.zeros((BLOCK, BLOCK), jnp.float32), unroll=2
            )
            src[it, me_c, pl.ds(q * step, step), :] = acc.T[:step, :]
            if remote:

                @pl.loop(1, n_cols)
                def _(d):
                    there = src.at[it, me_c, pl.ds(q * step, step)]
                    pltpu.make_async_remote_copy(
                        src_ref=there, dst_ref=there,
                        send_sem=src_send.at[it], recv_sem=src_recv.at[it, q],
                        device_id={"cols": lax.rem(me_c + d, n_cols)}, device_id_type=MESH,
                    ).start()

        for q in range(CHUNKS):
            if remote:
                landed = src.at[it, pl.ds(0, n_cols - 1), pl.ds(q * step, step)]
                pltpu.make_async_copy(landed, landed, src_recv.at[it, q]).wait()
            parts = src[it, :, pl.ds(q * step, step), :]
            peak = jnp.max(parts, axis=0)
            total = jnp.sum(jnp.exp2(parts - peak[None]), axis=0)
            phi = a_ref[pl.ds(q * step, step), :] * LOG2E - (peak + log2(total))
            f_ref[pl.ds(q * step, step), :] = UNIT * (phi + sqx[pl.ds(q * step, step), :])
            tall = jnp.concatenate([phi, jnp.zeros((BLOCK - step, BLOCK), jnp.float32)], axis=0).T

            @pl.loop(0, step, unroll=2)
            def _(k):
                b = q * step + k
                column = jnp.sum(jnp.where(lanes == k, tall, 0.0), axis=1, keepdims=True)
                for s in range(SLOTS):
                    scores = tile[b, :, s * BLOCK : (s + 1) * BLOCK] + column
                    peak = jnp.max(scores, axis=0, keepdims=True)
                    total = jnp.sum(jnp.exp2(scores - peak), axis=0, keepdims=True)
                    part[pl.ds(b * SLOTS + s, 1), :] = peak + log2(total)

        v = pick(first[...], part[...])
        for k, d in enumerate(SCAN):
            other = pltpu.roll(v, d, 0) + masks[k]
            peak = jnp.maximum(v, other)
            v = peak + log2(1.0 + jnp.exp2(jnp.minimum(v, other) - peak))
        v = pick(last[...], v) + hits[...]
        trg[it, :, :, :] = v.reshape(n_rows, share, BLOCK)
        if remote:

            @pl.loop(1, n_rows)
            def _(d):
                peer = lax.rem(me_r + d, n_rows)
                pltpu.make_async_remote_copy(
                    src_ref=trg.at[it, peer], dst_ref=landing.at[it, me_r],
                    send_sem=trg_send.at[it], recv_sem=trg_recv.at[it],
                    device_id={"rows": peer}, device_id_type=MESH,
                ).start()

        landing[it, me_r] = trg[it, me_r]
        if remote:
            landed = landing.at[it, pl.ds(0, n_rows - 1)]
            pltpu.make_async_copy(landed, landed, trg_recv.at[it]).wait()
        parts = landing[it]
        peak = jnp.max(parts, axis=0)
        total = jnp.sum(jnp.exp2(parts - peak[None]), axis=0)
        mass = b_ref[pl.ds(pl.multiple_of(me_r * share, share), share), :]
        own[it, me_r] = mass * LOG2E - (peak + log2(total))
        if remote:

            @pl.loop(1, n_rows)
            def _(d):
                pltpu.make_async_remote_copy(
                    src_ref=own.at[it, me_r], dst_ref=own.at[it, me_r],
                    send_sem=own_send.at[it], recv_sem=own_recv.at[it],
                    device_id={"rows": lax.rem(me_r + d, n_rows)}, device_id_type=MESH,
                ).start()

            landed = own.at[it, pl.ds(0, n_rows - 1)]
            pltpu.make_async_copy(landed, landed, own_recv.at[it]).wait()
        gam[pl.ds(0, tb), :] = own[it].reshape(tb, BLOCK)

    g_ref[...] = UNIT * (gam[pl.ds(0, tb), :] + sqy[...])
    if remote:
        for it in range(ITERS):
            sent = src.at[it, pl.ds(0, n_cols - 1)]
            pltpu.make_async_copy(sent, sent, src_send.at[it]).wait()
            sent = own.at[it, pl.ds(0, n_rows - 1)]
            pltpu.make_async_copy(sent, sent, own_send.at[it]).wait()
            pltpu.make_async_copy(sent, sent, trg_send.at[it]).wait()


def scratch(n_rows, n_cols, dim, sb, tb):
    f32, pairs = jnp.float32, sb * SLOTS
    dma = pltpu.SemaphoreType.DMA
    return [
        pltpu.VMEM((tb + 1, dim, BLOCK), jnp.bfloat16),
        pltpu.VMEM((sb, BLOCK, SLOTS * BLOCK), f32),
        pltpu.VMEM((tb + 8, BLOCK), f32),
        pltpu.VMEM((sb, BLOCK), f32),
        pltpu.VMEM((tb, BLOCK), f32),
        pltpu.VMEM((tb, BLOCK), f32),
        pltpu.VMEM((pairs, pairs), jnp.bfloat16),
        pltpu.VMEM((tb, pairs), jnp.bfloat16),
        pltpu.VMEM((len(SCAN), pairs, BLOCK), f32),
        pltpu.VMEM((pairs, BLOCK), f32),
        pltpu.VMEM((ITERS, n_cols, sb, BLOCK), f32),
        pltpu.VMEM((ITERS, n_rows, tb // n_rows, BLOCK), f32),
        pltpu.VMEM((ITERS, n_rows, tb // n_rows, BLOCK), f32),
        pltpu.VMEM((ITERS, n_rows, tb // n_rows, BLOCK), f32),
        dma,
        dma((ITERS,)),
        dma((ITERS, CHUNKS)),
        dma((ITERS,)),
        dma((ITERS,)),
        dma((ITERS,)),
        dma((ITERS,)),
    ]


def on_device(n_rows, n_cols, source_cells, target_cells, source_logmass, target_logmass, neighbours):
    sb = neighbours.shape[0]
    tb = target_cells.shape[1] // BLOCK
    pairs = sb * SLOTS
    local = neighbours - lax.axis_index("cols") * tb
    owned = (local >= 0) & (local < tb)
    upto = jnp.arange(LIST)[:, None] <= jnp.arange(LIST)[None, :]
    nth = jnp.sum(jnp.where(owned[:, :, None] & upto[None], 1, 0), axis=1)
    wanted = (nth[:, :, None] == 1 + jnp.arange(SLOTS)[None, None, :]) & owned[:, :, None]
    ids = tb + jnp.sum(jnp.where(wanted, local[:, :, None] - tb, 0), axis=1)
    ids = ids.reshape(pairs).astype(jnp.int32)
    vmem = pl.BlockSpec(memory_space=pltpu.VMEM)
    f, g = pl.pallas_call(
        functools.partial(kernel, n_rows, n_cols, True),
        out_shape=(
            jax.ShapeDtypeStruct((sb, BLOCK), jnp.float32),
            jax.ShapeDtypeStruct((tb, BLOCK), jnp.float32),
        ),
        in_specs=[pl.BlockSpec(memory_space=pltpu.SMEM), vmem, vmem, vmem]
        + [pl.BlockSpec(memory_space=pl.ANY), vmem, vmem],
        out_specs=(vmem, vmem),
        scratch_shapes=scratch(n_rows, n_cols, source_cells.shape[0], sb, tb),
        compiler_params=pltpu.CompilerParams(
            collective_id=0, has_side_effects=True, vmem_limit_bytes=48 * 2**20
        ),
        cost_estimate=pl.CostEstimate(
            flops=2 * pairs * 64 * BLOCK * BLOCK,
            bytes_accessed=2 * 64 * (sb + tb) * BLOCK,
            transcendentals=2 * ITERS * pairs * BLOCK * BLOCK,
        ),
    )(
        ids, ids.reshape(1, pairs), ids.reshape(pairs, 1), source_cells, target_cells,
        source_logmass.reshape(sb, BLOCK), target_logmass.reshape(tb, BLOCK),
    )
    return f.reshape(-1), g.reshape(-1)


def solution(mesh):
    placed = (P(None, "rows"), P(None, "cols"), P("rows"), P("cols"), P("rows", None))
    body = functools.partial(on_device, mesh.shape["rows"], mesh.shape["cols"])
    return jax.shard_map(
        body, mesh=mesh, in_specs=placed, out_specs=(P("rows"), P("cols")), check_vma=False
    )
```

time: 1330 us -> 123 us (0.09)
  waiting for transfers between devices: 799 us -> 0 us
  local copies, waits for them, and re-layouts: 203 us -> 6.74 us
  blocking collectives: 144 us -> 0 us
  Pallas kernels: 0 us -> 113 us
  other arithmetic: 81.6 us -> 1.63 us
  matrix products: 78.5 us -> 0 us
  between operations: 14.5 us -> 0.69 us
    psum x3 -> x0, waiting for transfers between devices: 425 us -> none  [on_device(): total_rows = lax.psum(summed * jnp.exp(block_peak - peak_rows), 'rows')]
    pmax x3 -> x0, waiting for transfers between devices: 374 us -> none  [on_device(): peak_rows = lax.pmax(block_peak, 'rows')]
    gather x128 -> x0, local copies, waits for them, and re-layouts: 182 us -> none  [the longest x48 136 us: tile_costs(): gathered = tgt_three[:, ids_in, :]]
    pallas_call x0 -> x1, Pallas kernels: none -> 113 us  [on_device(): pl.pallas_call(functools.partial(kernel, n_rows, n_cols, True), out_shape...]
    dot_general x48 -> x0, matrix products: 78.5 us -> none  [tile_costs(): jnp.einsum('dgi,dgsj->gisj', cells_in, gathered, preferred_element_type=j...]
    pmax x3 -> x0, blocking collectives: 72.6 us -> none  [on_device(): peak_all = lax.pmax(highest, 'cols')]
    psum x3 -> x0, blocking collectives: 71 us -> none  [on_device(): totals = lax.psum(totals * jnp.exp(highest - peak_all), 'cols')]
    scatter-add x3 -> x0, other arithmetic: 37.1 us -> none  [on_device(): summed = jax.ops.segment_sum(scaled, flat_ids, num_segments=tgt_blocks)]
  transfers between devices with their start and end apart: 6 -> 0, of which waited for: 6 -> 0; matrix products, arithmetic and copies ran while one was open for 3% -> 0% of each run, Pallas kernels for 0% -> 0%
where the time goes in v1:
time: 123 us; the launch traced here: 122 us
  Pallas kernels  113 us (92%)
  local copies, waits for them, and re-layouts  6.74 us (5%)
  other arithmetic  1.63 us (1%)
    pallas_call x1, Pallas kernels, on_device(): pl.pallas_call(functools.partial(kernel, n_rows, n_cols, True), out_shape...  113 us
    unnamed x10, local copies, waits for them, and re-layouts  6.35 us

profile of v1, /device:TPU:1, one launch (start us, length us, event | category | flops | bytes accessed | tf_op | source)
XLA Modules:
  0.0 121.6 jit_solution(15349448725378897724)
XLA Ops:
  0.6 0.7 compare_and_fusion
  1.4 0.1 select_reduce_fusion
  1.5 0.7 subtract_add_fusion
  2.2 0.1 select_reduce_fusion.1
  2.3 0.1 copy.14
  2.4 0.1 add.44.trow_ref
  2.5 0.1 add.43.ids_ref
  2.6 0.1 add.46.tcol_ref
  2.7 0.0 copy-start
  2.7 2.2 %copy-done = bf16[64,32768]{1,0:T(8,128)(2,1)S(1)} copy-done((bf16[64,32768]{1,0:T(8,128)(2,1)S(1)}, bf16[64,32768]{1,0:T(8,128)(2,1)}, u32[]{:S(2)}) %copy-start) | copy-done | bytes 4194328
  4.9 0.0 copy-start.1
  4.9 1.2 %copy-done.1 = bf16[64,8192]{1,0:T(8,128)(2,1)S(1)} copy-done((bf16[64,8192]{1,0:T(8,128)(2,1)S(1)}, bf16[64,8192]{1,0:T(8,128)(2,1)}, u32[]{:S(2)}) %copy-start.1) | copy-done | bytes 1048600
  6.1 0.0 copy-start.2
  6.1 0.9 copy-done.2
  7.0 0.0 copy-start.3
  7.0 0.8 copy-done.3
  7.8 112.5 %shard_map.68 = (f32[64,128]{1,0:T(8,128)S(1)}, f32[256,128]{1,0:T(8,128)S(1)}) custom-call(s32[256]{0:T(256)S(1)} %add.43.ids_ref, s32[1,256]{1,0:T(1,128)S(1)} %add.44.trow_ref, s32[256,1]{1,0:T(8,128)S(1)} %add.46.tcol_ref, bf16[64,8192]{1,0:T(8,128)(2,1)S(1)} %copy-done.1, bf16[64,32768]{1,0:T(8,128)(2,1)S(1)} %copy-done, f32[64,128]{1,0:T(8,128)S(1)} %bitcast.7, ...), custom_call_target="tpu_custom_call" | custom-call | flops 536870912 | bytes 5242880 | tf_op jit(solution)/shard_map/pallas_call | solution.py:274
  120.3 0.6 copy.20
  120.9 0.7 copy.21
  (3 shorter events, 0.0 us)
Async XLA Ops:
  2.7 2.2 %copy-start = (bf16[64,32768]{1,0:T(8,128)(2,1)S(1)}, bf16[64,32768]{1,0:T(8,128)(2,1)}, u32[]{:S(2)}) copy-start(bf16[64,32768]{1,0:T(8,128)(2,1)} %y_ref.1) | copy-start | bytes 12582916
  4.9 1.2 %copy-start.1 = (bf16[64,8192]{1,0:T(8,128)(2,1)S(1)}, bf16[64,8192]{1,0:T(8,128)(2,1)}, u32[]{:S(2)}) copy-start(bf16[64,8192]{1,0:T(8,128)(2,1)} %x_ref.1) | copy-start | bytes 3145732
  6.1 0.9 copy-start.2
  7.0 0.8 copy-start.3

commit v2 on v1

v2 whole, which is shorter than its diff:
```python
import functools
import math

import jax
import jax.numpy as jnp
from jax import lax
from jax.experimental import pallas as pl
from jax.experimental.pallas import tpu as pltpu
from jax.sharding import PartitionSpec as P

BLOCK = 128
SUB = 8
LIST = 16
ITERS = 3
SLOTS = 4
EPS = 0.05
NEG = -1e30
LOG2E = math.log2(math.e)
UNIT = EPS / LOG2E
CHUNKS = 4
GROUPS = 8
SCAN = (1, 2, 4, 8, 16, 32)
UNROLL = 8
MESH = pl.DeviceIdType.MESH


def log2(v):
    return jnp.log(v) * LOG2E


def tree(op, parts):
    parts = list(parts)
    while len(parts) > 1:
        pairs = [op(p, q) for p, q in zip(parts[::2], parts[1::2])]
        parts = pairs + parts[len(parts) // 2 * 2 :]
    return parts[0]


def thirds(v):
    high = v.astype(jnp.bfloat16).astype(jnp.float32)
    rest = v - high
    middle = rest.astype(jnp.bfloat16).astype(jnp.float32)
    return [high, middle, rest - middle]


def pick(onehot, v):
    parts = [p.astype(jnp.bfloat16) for p in thirds(v)]
    out = jnp.dot(onehot, jnp.concatenate(parts, axis=1), preferred_element_type=jnp.float32)
    return (out[:, :BLOCK] + out[:, BLOCK : 2 * BLOCK]) + out[:, 2 * BLOCK :]


def kernel(
    n_rows, n_cols, remote,
    ids_ref, trow_ref, tcol_ref, x_hbm, y_hbm, a_hbm, b_hbm,
    f_ref, g_ref,
    x_ref, cells_y, a_ref, b_ref, tile, gam, sqx, sqy, phi1, hits, first, last, hot, spread, masks,
    peaks, sums, columns, src, trg, landing, own,
    x_sem, y_sem, src_send, src_recv, trg_send, trg_recv, own_send, own_recv,
):
    dim = x_hbm.shape[0]
    kappa = 2.0 * LOG2E / (dim * EPS)
    sb, tb = x_hbm.shape[1] // BLOCK, y_hbm.shape[1] // BLOCK
    pairs = sb * SLOTS
    share = tb // n_rows
    step = sb // CHUNKS
    group = tb // GROUPS
    if remote:
        me_r, me_c = lax.axis_index("rows"), lax.axis_index("cols")
        barrier = pltpu.get_barrier_semaphore()

        @pl.loop(1, n_rows)
        def _(d):
            pl.semaphore_signal(
                barrier, inc=1, device_id={"rows": lax.rem(me_r + d, n_rows)}, device_id_type=MESH
            )

        @pl.loop(1, n_cols)
        def _(d):
            pl.semaphore_signal(
                barrier, inc=1, device_id={"cols": lax.rem(me_c + d, n_cols)}, device_id_type=MESH
            )
    else:
        me_r = me_c = 0

    for n in range(GROUPS):

        @pl.loop(0, group, unroll=8)
        def _(k):
            t = n * group + k
            pltpu.make_async_copy(
                y_hbm.at[:, pl.ds(pl.multiple_of(t * BLOCK, BLOCK), BLOCK)],
                cells_y.at[t], y_sem.at[n],
            ).start()

    mass = b_hbm.at[pl.ds(pl.multiple_of(me_r * share, share), share)]
    fetch = [
        pltpu.make_async_copy(x_hbm, x_ref, x_sem.at[0]),
        pltpu.make_async_copy(a_hbm, a_ref, x_sem.at[1]),
        pltpu.make_async_copy(mass, b_ref, x_sem.at[2]),
    ]
    for copy in fetch:
        copy.start()

    tr, tc = trow_ref[...], tcol_ref[...]
    ip = lax.broadcasted_iota(jnp.int32, (pairs, pairs), 0)
    iq = lax.broadcasted_iota(jnp.int32, (pairs, pairs), 1)
    before = (tc < tr) | ((tc == tr) & (ip < iq))
    place = jnp.sum(jnp.where(before, 1.0, 0.0), axis=0, keepdims=True)
    put = place == ip.astype(jnp.float32)
    first[...] = jnp.where(put, 1.0, 0.0).astype(jnp.bfloat16)
    trf = tr.astype(jnp.float32)
    ordered = jnp.sum(jnp.where(put, trf, 0.0), axis=1, keepdims=True)
    it_ = lax.broadcasted_iota(jnp.int32, (tb, pairs), 0)
    iu = lax.broadcasted_iota(jnp.int32, (tb, pairs), 1)
    same = jnp.where(tr == it_, 1.0, 0.0)
    hot[...] = same.astype(jnp.bfloat16)
    upto = jnp.sum(jnp.where(tr <= it_, 1.0, 0.0), axis=1, keepdims=True)
    count = jnp.sum(same, axis=1, keepdims=True)
    at = jnp.where(count > 0.0, upto - 1.0, -1.0)
    last[...] = jnp.where(iu.astype(jnp.float32) == at, 1.0, 0.0).astype(jnp.bfloat16)
    hits[...] = jnp.broadcast_to(jnp.where(count > 0.0, 0.0, NEG), (tb, BLOCK))
    wide = jnp.broadcast_to(ordered, (pairs, BLOCK))
    rows = lax.broadcasted_iota(jnp.int32, (pairs, BLOCK), 0)
    for k, d in enumerate(SCAN):
        joined = (wide == pltpu.roll(wide, d, 0)) & (rows >= d)
        masks[k] = jnp.where(joined, 0.0, NEG)
    ik = lax.broadcasted_iota(jnp.int32, (BLOCK, step * BLOCK), 0)
    ib = lax.broadcasted_iota(jnp.int32, (BLOCK, step * BLOCK), 1) // BLOCK
    chosen = (ik == ib) | (ik == ib + step) | (ik == ib + 2 * step)
    spread[...] = jnp.where(chosen, 1.0, 0.0).astype(jnp.bfloat16)

    cells_y[tb] = jnp.zeros((dim, BLOCK), jnp.bfloat16)
    gam[pl.ds(tb, SUB), :] = jnp.full((SUB, BLOCK), NEG, jnp.float32)
    for n in range(GROUPS):
        landed = cells_y.at[pl.ds(n * group, group)]
        pltpu.make_async_copy(landed, landed, y_sem.at[n]).wait()

        @pl.loop(0, group, unroll=UNROLL)
        def _(k):
            t = n * group + k
            cells = cells_y[t].astype(jnp.float32)
            squares = jnp.sum(cells * cells, axis=0, keepdims=True) * (0.5 * kappa)
            sqy[pl.ds(t, 1), :] = squares
            gam[pl.ds(t, 1), :] = -squares

    for copy in fetch:
        copy.wait()

    @pl.loop(0, sb, unroll=UNROLL)
    def _(b):
        cells = x_ref[:, pl.ds(pl.multiple_of(b * BLOCK, BLOCK), BLOCK)].astype(jnp.float32)
        sqx[pl.ds(b, 1), :] = jnp.sum(cells * cells, axis=0, keepdims=True) * (0.5 * kappa)

    def send_rows(it, q):
        if remote:

            @pl.loop(1, n_cols)
            def _(d):
                there = src.at[it, me_c, pl.ds(q * step, step)]
                pltpu.make_async_remote_copy(
                    src_ref=there, dst_ref=there,
                    send_sem=src_send.at[it], recv_sem=src_recv.at[it, q],
                    device_id={"cols": lax.rem(me_c + d, n_cols)}, device_id_type=MESH,
                ).start()

    def rows_landed(it, q):
        if remote:
            landed = src.at[it, pl.ds(0, n_cols - 1), pl.ds(q * step, step)]
            pltpu.make_async_copy(landed, landed, src_recv.at[it, q]).wait()
        return src[it, :, pl.ds(q * step, step), :]

    def to_columns(v):
        parts = jnp.concatenate(
            thirds(v) + [jnp.zeros((BLOCK - 3 * step, BLOCK), jnp.float32)], axis=0
        )
        tall = parts.T.astype(jnp.bfloat16)
        for k in range(0, step, 2):
            both = jnp.dot(
                tall, spread[:, k * BLOCK : (k + 2) * BLOCK], preferred_element_type=jnp.float32
            )
            columns[k] = both[:, :BLOCK]
            columns[k + 1] = both[:, BLOCK:]

    def sum_rows(it, v, combine):
        trg[it] = v.reshape(n_rows, share, BLOCK)
        if remote:

            @pl.loop(1, n_rows)
            def _(d):
                peer = lax.rem(me_r + d, n_rows)
                pltpu.make_async_remote_copy(
                    src_ref=trg.at[it, peer], dst_ref=landing.at[it, me_r],
                    send_sem=trg_send.at[it], recv_sem=trg_recv.at[it],
                    device_id={"rows": peer}, device_id_type=MESH,
                ).start()

        landing[it, me_r] = trg[it, me_r]
        if remote:
            landed = landing.at[it, pl.ds(0, n_rows - 1)]
            pltpu.make_async_copy(landed, landed, trg_recv.at[it]).wait()
        own[it, me_r] = combine(landing[it])
        if remote:

            @pl.loop(1, n_rows)
            def _(d):
                pltpu.make_async_remote_copy(
                    src_ref=own.at[it, me_r], dst_ref=own.at[it, me_r],
                    send_sem=own_send.at[it], recv_sem=own_recv.at[it],
                    device_id={"rows": lax.rem(me_r + d, n_rows)}, device_id_type=MESH,
                ).start()

            landed = own.at[it, pl.ds(0, n_rows - 1)]
            pltpu.make_async_copy(landed, landed, own_recv.at[it]).wait()
        return own[it].reshape(tb, BLOCK)

    def strips(b, s):
        return [tile[b, r : r + SUB, s * BLOCK : (s + 1) * BLOCK] for r in range(0, BLOCK, SUB)]

    def column(k):
        return [columns[k, r : r + SUB, :] for r in range(0, BLOCK, SUB)]

    def place_at(p):
        return pl.ds(pl.multiple_of(p * SUB, SUB), SUB)

    def folded(ref):
        return [ref[pl.ds(k, pairs, stride=SUB), :] for k in range(SUB)]

    for q in range(CHUNKS):

        @pl.loop(0, step, unroll=UNROLL // 2)
        def _(k):
            b = q * step + k
            cells = x_ref[:, pl.ds(pl.multiple_of(b * BLOCK, BLOCK), BLOCK)]
            ids = [ids_ref[b * SLOTS + s] for s in range(SLOTS)]
            crossed = lax.dot_general(
                cells, jnp.concatenate([cells_y[t] for t in ids], axis=1), (((0,), (0,)), ((), ())),
                preferred_element_type=jnp.float32,
            )
            tile[b] = crossed * kappa
            starts = [gam[t][None, :] for t in ids]
            logs = []
            for r in range(0, BLOCK, 4 * SUB):
                scores = [
                    tile[b, r : r + 4 * SUB, s * BLOCK : (s + 1) * BLOCK] + starts[s]
                    for s in range(SLOTS)
                ]
                peak = tree(jnp.maximum, scores)
                logs.append(peak + log2(tree(jnp.add, [jnp.exp2(v - peak) for v in scores])))
            logs = jnp.concatenate(logs, axis=0).T
            peak = jnp.max(logs, axis=0, keepdims=True)
            total = jnp.sum(jnp.exp2(logs - peak), axis=0, keepdims=True)
            src[0, me_c, pl.ds(b, 1), :] = peak + log2(total)

        if remote and q == 0:
            pl.semaphore_wait(barrier, n_rows + n_cols - 2)
        send_rows(0, q)

    for q in range(CHUNKS):
        here = pl.ds(q * step, step)
        parts = rows_landed(0, q)
        peak = jnp.max(parts, axis=0)
        total = jnp.sum(jnp.exp2(parts - peak[None]), axis=0)
        phi = a_ref[here, :] * LOG2E - (peak + log2(total))
        phi1[here, :] = phi
        to_columns(phi)

        @pl.loop(0, step, unroll=UNROLL // 2)
        def _(k):
            b = q * step + k
            phis = column(k)
            for s in range(SLOTS):
                scores = [v + c for v, c in zip(strips(b, s), phis)]
                peak = tree(jnp.maximum, scores)
                exps = [jnp.exp2(v - peak) for v in scores]
                for r, e in enumerate(exps):
                    tile[b, r * SUB : (r + 1) * SUB, s * BLOCK : (s + 1) * BLOCK] = e
                peaks[place_at(b * SLOTS + s), :] = peak
                sums[place_at(b * SLOTS + s), :] = tree(jnp.add, exps)

    tops = folded(peaks)
    peak = tree(jnp.maximum, tops)
    total = tree(jnp.add, [v * jnp.exp2(p - peak) for v, p in zip(folded(sums), tops)])
    v = pick(first[...], peak + log2(total))
    for k, d in enumerate(SCAN):
        other = pltpu.roll(v, d, 0) + masks[k]
        peak = jnp.maximum(v, other)
        v = peak + log2(1.0 + jnp.exp2(jnp.minimum(v, other) - peak))

    def combine_logs(parts):
        peak = jnp.max(parts, axis=0)
        total = jnp.sum(jnp.exp2(parts - peak[None]), axis=0)
        return b_ref[...] * LOG2E - (peak + log2(total))

    gam[pl.ds(0, tb), :] = sum_rows(0, pick(last[...], v) + hits[...], combine_logs)

    @pl.loop(0, pairs, unroll=UNROLL)
    def _(p):
        peaks[place_at(p), :] = jnp.exp2(peaks[place_at(p), :] + gam[ids_ref[p]][None, :])

    gam[...] = jnp.ones(gam.shape, jnp.float32)

    lanes = lax.broadcasted_iota(jnp.int32, (BLOCK, BLOCK), 1)

    @pl.loop(1, ITERS)
    def _(it):
        for q in range(CHUNKS):

            def source_block(k, acc):
                b = q * step + k
                weights = [
                    peaks[place_at(b * SLOTS + s), :] * gam[ids_ref[b * SLOTS + s]][None, :]
                    for s in range(SLOTS)
                ]
                tiles = [strips(b, s) for s in range(SLOTS)]
                total = jnp.concatenate(
                    [
                        tree(jnp.add, [tiles[s][r] * weights[s] for s in range(SLOTS)])
                        for r in range(BLOCK // SUB)
                    ],
                    axis=0,
                )
                return jnp.where(lanes == k, jnp.sum(total, axis=1, keepdims=True), acc)

            acc = lax.fori_loop(
                0, step, source_block, jnp.zeros((BLOCK, BLOCK), jnp.float32), unroll=UNROLL
            )
            src[it, me_c, pl.ds(q * step, step), :] = acc.T[:step, :]
            send_rows(it, q)

        for q in range(CHUNKS):
            here = pl.ds(q * step, step)
            factor = jnp.exp(a_ref[here, :]) / jnp.sum(rows_landed(it, q), axis=0)
            f_ref[here, :] = UNIT * ((phi1[here, :] + sqx[here, :]) + log2(factor))
            to_columns(factor)

            @pl.loop(0, step, unroll=UNROLL)
            def _(k):
                b = q * step + k
                factors = column(k)
                for s in range(SLOTS):
                    total = tree(jnp.add, [v * c for v, c in zip(strips(b, s), factors)])
                    here = place_at(b * SLOTS + s)
                    sums[here, :] = total * peaks[here, :]

        gam[pl.ds(0, tb), :] = sum_rows(
            it,
            pick(hot[...], tree(jnp.add, folded(sums))),
            lambda parts: jnp.exp(b_ref[...]) / jnp.sum(parts, axis=0),
        )

    g_ref[...] = UNIT * ((own[0].reshape(tb, BLOCK) + sqy[...]) + log2(gam[pl.ds(0, tb), :]))
    if remote:
        for it in range(ITERS):
            sent = src.at[it, pl.ds(0, n_cols - 1)]
            pltpu.make_async_copy(sent, sent, src_send.at[it]).wait()
            sent = own.at[it, pl.ds(0, n_rows - 1)]
            pltpu.make_async_copy(sent, sent, own_send.at[it]).wait()
            pltpu.make_async_copy(sent, sent, trg_send.at[it]).wait()


def scratch(n_rows, n_cols, dim, sb, tb):
    f32, bf16, pairs = jnp.float32, jnp.bfloat16, sb * SLOTS
    dma = pltpu.SemaphoreType.DMA
    shared = (ITERS, n_rows, tb // n_rows, BLOCK)
    return [
        pltpu.VMEM((dim, sb * BLOCK), bf16),
        pltpu.VMEM((tb + 1, dim, BLOCK), bf16),
        pltpu.VMEM((sb, BLOCK), f32),
        pltpu.VMEM((tb // n_rows, BLOCK), f32),
        pltpu.VMEM((sb, BLOCK, SLOTS * BLOCK), f32),
        pltpu.VMEM((tb + SUB, BLOCK), f32),
        pltpu.VMEM((sb, BLOCK), f32),
        pltpu.VMEM((tb, BLOCK), f32),
        pltpu.VMEM((sb, BLOCK), f32),
        pltpu.VMEM((tb, BLOCK), f32),
        pltpu.VMEM((pairs, pairs), bf16),
        pltpu.VMEM((tb, pairs), bf16),
        pltpu.VMEM((tb, pairs), bf16),
        pltpu.VMEM((BLOCK, sb // CHUNKS * BLOCK), bf16),
        pltpu.VMEM((len(SCAN), pairs, BLOCK), f32),
        pltpu.VMEM((pairs * SUB, BLOCK), f32),
        pltpu.VMEM((pairs * SUB, BLOCK), f32),
        pltpu.VMEM((sb // CHUNKS, BLOCK, BLOCK), f32),
        pltpu.VMEM((ITERS, n_cols, sb, BLOCK), f32),
        pltpu.VMEM(shared, f32),
        pltpu.VMEM(shared, f32),
        pltpu.VMEM(shared, f32),
        dma((3,)),
        dma((GROUPS,)),
        dma((ITERS,)),
        dma((ITERS, CHUNKS)),
        dma((ITERS,)),
        dma((ITERS,)),
        dma((ITERS,)),
        dma((ITERS,)),
    ]


def make_call(n_rows, n_cols, dim, sb, tb, remote=True):
    pairs = sb * SLOTS
    vmem = pl.BlockSpec(memory_space=pltpu.VMEM)
    return pl.pallas_call(
        functools.partial(kernel, n_rows, n_cols, remote),
        out_shape=(
            jax.ShapeDtypeStruct((sb, BLOCK), jnp.float32),
            jax.ShapeDtypeStruct((tb, BLOCK), jnp.float32),
        ),
        in_specs=[pl.BlockSpec(memory_space=pltpu.SMEM), vmem, vmem]
        + [pl.BlockSpec(memory_space=pl.ANY)] * 4,
        out_specs=(vmem, vmem),
        scratch_shapes=scratch(n_rows, n_cols, dim, sb, tb),
        compiler_params=pltpu.CompilerParams(
            collective_id=0 if remote else None, has_side_effects=True, vmem_limit_bytes=48 * 2**20
        ),
        cost_estimate=pl.CostEstimate(
            flops=2 * pairs * dim * BLOCK * BLOCK,
            bytes_accessed=2 * dim * (sb + tb) * BLOCK,
            transcendentals=2 * pairs * BLOCK * BLOCK,
        ),
    )


def on_device(n_rows, n_cols, source_cells, target_cells, source_logmass, target_logmass, neighbours):
    sb = neighbours.shape[0]
    tb = target_cells.shape[1] // BLOCK
    pairs = sb * SLOTS
    local = neighbours - lax.axis_index("cols") * tb
    owned = (local >= 0) & (local < tb)
    upto = jnp.arange(LIST)[:, None] <= jnp.arange(LIST)[None, :]
    nth = jnp.sum(jnp.where(owned[:, :, None] & upto[None], 1, 0), axis=1)
    wanted = (nth[:, :, None] == 1 + jnp.arange(SLOTS)[None, None, :]) & owned[:, :, None]
    ids = tb + jnp.sum(jnp.where(wanted, local[:, :, None] - tb, 0), axis=1)
    ids = ids.reshape(pairs).astype(jnp.int32)
    f, g = make_call(n_rows, n_cols, source_cells.shape[0], sb, tb)(
        ids, ids.reshape(1, pairs), ids.reshape(pairs, 1), source_cells, target_cells,
        source_logmass.reshape(sb, BLOCK), target_logmass.reshape(tb, BLOCK),
    )
    return f.reshape(-1), g.reshape(-1)


def solution(mesh):
    placed = (P(None, "rows"), P(None, "cols"), P("rows"), P("cols"), P("rows", None))
    body = functools.partial(on_device, mesh.shape["rows"], mesh.shape["cols"])
    return jax.shard_map(
        body, mesh=mesh, in_specs=placed, out_specs=(P("rows"), P("cols")), check_vma=False
    )
```

time: 123 us -> 94.9 us (0.77)
  Pallas kernels: 113 us -> 85.5 us
    pallas_call x1, Pallas kernels: 113 us -> 85.5 us  [on_device(): make_call(n_rows, n_cols, source_cells.shape[0], sb, tb)]
where the time goes in v2:
time: 94.9 us; the launch traced here: 94.6 us
  Pallas kernels  85.5 us (90%)
  local copies, waits for them, and re-layouts  6.74 us (7%)
  other arithmetic  1.63 us (2%)
    pallas_call x1, Pallas kernels, on_device(): make_call(n_rows, n_cols, source_cells.shape[0], sb, tb)  85.5 us
    unnamed x10, local copies, waits for them, and re-layouts  6.35 us

profile of v2, /device:TPU:1, one launch (start us, length us, event | category | flops | bytes accessed | tf_op | source)
XLA Modules:
  0.0 94.6 jit_solution(17896978716521978620)
XLA Ops:
  0.6 0.7 compare_and_fusion
  1.4 0.1 select_reduce_fusion
  1.5 0.7 subtract_add_fusion
  2.2 0.1 select_reduce_fusion.1
  2.3 0.1 copy.14
  2.4 0.1 add.44.trow_ref
  2.5 0.1 add.43.ids_ref
  2.6 0.1 add.46.tcol_ref
  2.7 0.0 copy-start
  2.7 2.2 %copy-done = bf16[64,32768]{1,0:T(8,128)(2,1)S(1)} copy-done((bf16[64,32768]{1,0:T(8,128)(2,1)S(1)}, bf16[64,32768]{1,0:T(8,128)(2,1)}, u32[]{:S(2)}) %copy-start) | copy-done | bytes 4194328
  4.9 0.0 copy-start.1
  4.9 1.2 %copy-done.1 = bf16[64,8192]{1,0:T(8,128)(2,1)S(1)} copy-done((bf16[64,8192]{1,0:T(8,128)(2,1)S(1)}, bf16[64,8192]{1,0:T(8,128)(2,1)}, u32[]{:S(2)}) %copy-start.1) | copy-done | bytes 1048600
  6.1 0.0 copy-start.2
  6.1 0.9 copy-done.2
  7.0 0.0 copy-start.3
  7.0 0.8 copy-done.3
  7.8 85.5 %shard_map.68 = (f32[64,128]{1,0:T(8,128)S(1)}, f32[256,128]{1,0:T(8,128)S(1)}) custom-call(s32[256]{0:T(256)S(1)} %add.43.ids_ref, s32[1,256]{1,0:T(1,128)S(1)} %add.44.trow_ref, s32[256,1]{1,0:T(8,128)S(1)} %add.46.tcol_ref, bf16[64,8192]{1,0:T(8,128)(2,1)S(1)} %copy-done.1, bf16[64,32768]{1,0:T(8,128)(2,1)S(1)} %copy-done, f32[64,128]{1,0:T(8,128)S(1)} %bitcast.7, ...), custom_call_target="tpu_custom_call" | custom-call | flops 536870912 | bytes 5242880 | tf_op jit(solution)/shard_map/pallas_call | solution.py:434
  93.3 0.6 copy.20
  93.9 0.7 copy.21
  (3 shorter events, 0.0 us)
Async XLA Ops:
  2.7 2.2 %copy-start = (bf16[64,32768]{1,0:T(8,128)(2,1)S(1)}, bf16[64,32768]{1,0:T(8,128)(2,1)}, u32[]{:S(2)}) copy-start(bf16[64,32768]{1,0:T(8,128)(2,1)} %y_hbm.1) | copy-start | bytes 12582916
  4.9 1.2 %copy-start.1 = (bf16[64,8192]{1,0:T(8,128)(2,1)S(1)}, bf16[64,8192]{1,0:T(8,128)(2,1)}, u32[]{:S(2)}) copy-start(bf16[64,8192]{1,0:T(8,128)(2,1)} %x_hbm.1) | copy-start | bytes 3145732
  6.1 0.9 copy-start.2
  7.0 0.8 copy-start.3

commit v3 on v2

--- a/solution.py
+++ b/solution.py
@@ -20,7 +20,7 @@
 CHUNKS = 4
 GROUPS = 8
 SCAN = (1, 2, 4, 8, 16, 32)
-UNROLL = 8
+UNROLL = 16
 MESH = pl.DeviceIdType.MESH
 
 
@@ -51,11 +51,10 @@
 
 def kernel(
     n_rows, n_cols, remote,
-    ids_ref, trow_ref, tcol_ref, x_hbm, y_hbm, a_hbm, b_hbm,
+    x_hbm, y_hbm, a_hbm, b_hbm, n_hbm,
     f_ref, g_ref,
-    x_ref, cells_y, a_ref, b_ref, tile, gam, sqx, sqy, phi1, hits, first, last, hot, spread, masks,
-    peaks, sums, columns, src, trg, landing, own,
-    x_sem, y_sem, src_send, src_recv, trg_send, trg_recv, own_send, own_recv,
+    n_ref, listed, ids_ref, x_ref, cells_y, a_ref, b_ref, tile, gam, sqx, sqy, phi1, hits, first, last,
+    hot, masks, peaks, sums, src, trg, landing, own, x_sem, y_sem, src_send, src_recv, trg_send, trg_recv, own_send, own_recv,
 ):
     dim = x_hbm.shape[0]
     kappa = 2.0 * LOG2E / (dim * EPS)
@@ -82,6 +81,8 @@
     else:
         me_r = me_c = 0
 
+    fetch_lists = pltpu.make_async_copy(n_hbm, n_ref, x_sem.at[3])
+    fetch_lists.start()
     for n in range(GROUPS):
 
         @pl.loop(0, group, unroll=8)
@@ -101,16 +102,37 @@
     for copy in fetch:
         copy.start()
 
-    tr, tc = trow_ref[...], tcol_ref[...]
+    fetch_lists.wait()
+    local = n_ref[...] - me_c * tb
+    owned = (local >= 0) & (local < tb)
+    ik = lax.broadcasted_iota(jnp.int32, (LIST, LIST), 0)
+    il = lax.broadcasted_iota(jnp.int32, (LIST, LIST), 1)
+    nth = jnp.dot(
+        jnp.where(owned, 1.0, 0.0).astype(jnp.bfloat16),
+        jnp.where(ik <= il, 1.0, 0.0).astype(jnp.bfloat16),
+        preferred_element_type=jnp.float32,
+    )
+    away = local.astype(jnp.float32) - tb
+    slots = [
+        jnp.sum(jnp.where(owned & (nth == s + 1.0), away, 0.0), axis=1, keepdims=True) + tb
+        for s in range(SLOTS)
+    ]
+    at_lane = lax.broadcasted_iota(jnp.int32, (sb, BLOCK), 1)
+    ids = sum(jnp.where(at_lane == s, slots[s], 0.0) for s in range(SLOTS)).astype(jnp.int32)
+    listed[...] = jnp.minimum(jnp.maximum(ids, 0), tb)
+    to_scalars = pltpu.make_async_copy(listed, ids_ref, x_sem.at[4])
+    to_scalars.start()
+
+    tc = jnp.concatenate(slots, axis=0)
     ip = lax.broadcasted_iota(jnp.int32, (pairs, pairs), 0)
     iq = lax.broadcasted_iota(jnp.int32, (pairs, pairs), 1)
+    tr = jnp.sum(jnp.where(ip == iq, tc, 0.0), axis=0, keepdims=True)
     before = (tc < tr) | ((tc == tr) & (ip < iq))
     place = jnp.sum(jnp.where(before, 1.0, 0.0), axis=0, keepdims=True)
     put = place == ip.astype(jnp.float32)
     first[...] = jnp.where(put, 1.0, 0.0).astype(jnp.bfloat16)
-    trf = tr.astype(jnp.float32)
-    ordered = jnp.sum(jnp.where(put, trf, 0.0), axis=1, keepdims=True)
-    it_ = lax.broadcasted_iota(jnp.int32, (tb, pairs), 0)
+    ordered = jnp.sum(jnp.where(put, tr, 0.0), axis=1, keepdims=True)
+    it_ = lax.broadcasted_iota(jnp.int32, (tb, pairs), 0).astype(jnp.float32)
     iu = lax.broadcasted_iota(jnp.int32, (tb, pairs), 1)
     same = jnp.where(tr == it_, 1.0, 0.0)
     hot[...] = same.astype(jnp.bfloat16)
@@ -124,11 +146,6 @@
     for k, d in enumerate(SCAN):
         joined = (wide == pltpu.roll(wide, d, 0)) & (rows >= d)
         masks[k] = jnp.where(joined, 0.0, NEG)
-    ik = lax.broadcasted_iota(jnp.int32, (BLOCK, step * BLOCK), 0)
-    ib = lax.broadcasted_iota(jnp.int32, (BLOCK, step * BLOCK), 1) // BLOCK
-    chosen = (ik == ib) | (ik == ib + step) | (ik == ib + 2 * step)
-    spread[...] = jnp.where(chosen, 1.0, 0.0).astype(jnp.bfloat16)
-
     cells_y[tb] = jnp.zeros((dim, BLOCK), jnp.bfloat16)
     gam[pl.ds(tb, SUB), :] = jnp.full((SUB, BLOCK), NEG, jnp.float32)
     for n in range(GROUPS):
@@ -151,12 +168,15 @@
         cells = x_ref[:, pl.ds(pl.multiple_of(b * BLOCK, BLOCK), BLOCK)].astype(jnp.float32)
         sqx[pl.ds(b, 1), :] = jnp.sum(cells * cells, axis=0, keepdims=True) * (0.5 * kappa)
 
+    def chunk(q):
+        return pl.ds(pl.multiple_of(q * step, step), step)
+
     def send_rows(it, q):
         if remote:
 
             @pl.loop(1, n_cols)
             def _(d):
-                there = src.at[it, me_c, pl.ds(q * step, step)]
+                there = src.at[it, me_c, chunk(q)]
                 pltpu.make_async_remote_copy(
                     src_ref=there, dst_ref=there,
                     send_sem=src_send.at[it], recv_sem=src_recv.at[it, q],
@@ -165,21 +185,13 @@
 
     def rows_landed(it, q):
         if remote:
-            landed = src.at[it, pl.ds(0, n_cols - 1), pl.ds(q * step, step)]
+            landed = src.at[it, pl.ds(0, n_cols - 1), chunk(q)]
             pltpu.make_async_copy(landed, landed, src_recv.at[it, q]).wait()
-        return src[it, :, pl.ds(q * step, step), :]
+        return src[it, :, chunk(q), :]
 
     def to_columns(v):
-        parts = jnp.concatenate(
-            thirds(v) + [jnp.zeros((BLOCK - 3 * step, BLOCK), jnp.float32)], axis=0
-        )
-        tall = parts.T.astype(jnp.bfloat16)
-        for k in range(0, step, 2):
-            both = jnp.dot(
-                tall, spread[:, k * BLOCK : (k + 2) * BLOCK], preferred_element_type=jnp.float32
-            )
-            columns[k] = both[:, :BLOCK]
-            columns[k + 1] = both[:, BLOCK:]
+        tall = jnp.concatenate([v, jnp.zeros((BLOCK - step, BLOCK), jnp.float32)], axis=0).T
+        return [jnp.broadcast_to(tall[:, k : k + 1], (BLOCK, BLOCK)) for k in range(step)]
 
     def sum_rows(it, v, combine):
         trg[it] = v.reshape(n_rows, share, BLOCK)
@@ -216,8 +228,8 @@
     def strips(b, s):
         return [tile[b, r : r + SUB, s * BLOCK : (s + 1) * BLOCK] for r in range(0, BLOCK, SUB)]
 
-    def column(k):
-        return [columns[k, r : r + SUB, :] for r in range(0, BLOCK, SUB)]
+    def cut(v):
+        return [v[r : r + SUB, :] for r in range(0, BLOCK, SUB)]
 
     def place_at(p):
         return pl.ds(pl.multiple_of(p * SUB, SUB), SUB)
@@ -225,23 +237,26 @@
     def folded(ref):
         return [ref[pl.ds(k, pairs, stride=SUB), :] for k in range(SUB)]
 
-    for q in range(CHUNKS):
-
-        @pl.loop(0, step, unroll=UNROLL // 2)
+    to_scalars.wait()
+
+    @pl.loop(0, CHUNKS)
+    def _(q):
+        @pl.loop(0, step, unroll=UNROLL)
         def _(k):
             b = q * step + k
             cells = x_ref[:, pl.ds(pl.multiple_of(b * BLOCK, BLOCK), BLOCK)]
-            ids = [ids_ref[b * SLOTS + s] for s in range(SLOTS)]
+            ids = [ids_ref[b, s] for s in range(SLOTS)]
             crossed = lax.dot_general(
                 cells, jnp.concatenate([cells_y[t] for t in ids], axis=1), (((0,), (0,)), ((), ())),
                 preferred_element_type=jnp.float32,
             )
-            tile[b] = crossed * kappa
+            crossed = crossed * kappa
+            tile[b] = crossed
             starts = [gam[t][None, :] for t in ids]
             logs = []
             for r in range(0, BLOCK, 4 * SUB):
                 scores = [
-                    tile[b, r : r + 4 * SUB, s * BLOCK : (s + 1) * BLOCK] + starts[s]
+                    crossed[r : r + 4 * SUB, s * BLOCK : (s + 1) * BLOCK] + starts[s]
                     for s in range(SLOTS)
                 ]
                 peak = tree(jnp.maximum, scores)
@@ -251,31 +266,33 @@
             total = jnp.sum(jnp.exp2(logs - peak), axis=0, keepdims=True)
             src[0, me_c, pl.ds(b, 1), :] = peak + log2(total)
 
-        if remote and q == 0:
-            pl.semaphore_wait(barrier, n_rows + n_cols - 2)
+        if remote:
+
+            @pl.when(q == 0)
+            def _():
+                pl.semaphore_wait(barrier, n_rows + n_cols - 2)
+
         send_rows(0, q)
 
-    for q in range(CHUNKS):
-        here = pl.ds(q * step, step)
+    @pl.loop(0, CHUNKS)
+    def _(q):
+        here = chunk(q)
         parts = rows_landed(0, q)
         peak = jnp.max(parts, axis=0)
         total = jnp.sum(jnp.exp2(parts - peak[None]), axis=0)
         phi = a_ref[here, :] * LOG2E - (peak + log2(total))
         phi1[here, :] = phi
-        to_columns(phi)
-
-        @pl.loop(0, step, unroll=UNROLL // 2)
-        def _(k):
+        for k, phis in enumerate(to_columns(phi)):
             b = q * step + k
-            phis = column(k)
+            phis = cut(phis)
             for s in range(SLOTS):
                 scores = [v + c for v, c in zip(strips(b, s), phis)]
                 peak = tree(jnp.maximum, scores)
                 exps = [jnp.exp2(v - peak) for v in scores]
                 for r, e in enumerate(exps):
                     tile[b, r * SUB : (r + 1) * SUB, s * BLOCK : (s + 1) * BLOCK] = e
-                peaks[place_at(b * SLOTS + s), :] = peak
-                sums[place_at(b * SLOTS + s), :] = tree(jnp.add, exps)
+                peaks[place_at(s * sb + b), :] = peak
+                sums[place_at(s * sb + b), :] = tree(jnp.add, exps)
 
     tops = folded(peaks)
     peak = tree(jnp.maximum, tops)
@@ -293,24 +310,22 @@
 
     gam[pl.ds(0, tb), :] = sum_rows(0, pick(last[...], v) + hits[...], combine_logs)
 
-    @pl.loop(0, pairs, unroll=UNROLL)
-    def _(p):
-        peaks[place_at(p), :] = jnp.exp2(peaks[place_at(p), :] + gam[ids_ref[p]][None, :])
-
-    gam[...] = jnp.ones(gam.shape, jnp.float32)
-
     lanes = lax.broadcasted_iota(jnp.int32, (BLOCK, BLOCK), 1)
-
-    @pl.loop(1, ITERS)
-    def _(it):
-        for q in range(CHUNKS):
-
+    for it in range(1, ITERS):
+
+        @pl.loop(0, CHUNKS)
+        def _(q):
             def source_block(k, acc):
                 b = q * step + k
-                weights = [
-                    peaks[place_at(b * SLOTS + s), :] * gam[ids_ref[b * SLOTS + s]][None, :]
-                    for s in range(SLOTS)
-                ]
+                weights = []
+                for s in range(SLOTS):
+                    here = place_at(s * sb + b)
+                    row = gam[ids_ref[b, s]][None, :]
+                    if it == 1:
+                        peaks[here, :] = jnp.exp2(peaks[here, :] + row)
+                        weights.append(peaks[here, :])
+                    else:
+                        weights.append(peaks[here, :] * row)
                 tiles = [strips(b, s) for s in range(SLOTS)]
                 total = jnp.concatenate(
                     [
@@ -324,23 +339,21 @@
             acc = lax.fori_loop(
                 0, step, source_block, jnp.zeros((BLOCK, BLOCK), jnp.float32), unroll=UNROLL
             )
-            src[it, me_c, pl.ds(q * step, step), :] = acc.T[:step, :]
+            src[it, me_c, chunk(q), :] = acc.T[:step, :]
             send_rows(it, q)
 
-        for q in range(CHUNKS):
-            here = pl.ds(q * step, step)
+        @pl.loop(0, CHUNKS)
+        def _(q):
+            here = chunk(q)
             factor = jnp.exp(a_ref[here, :]) / jnp.sum(rows_landed(it, q), axis=0)
             f_ref[here, :] = UNIT * ((phi1[here, :] + sqx[here, :]) + log2(factor))
-            to_columns(factor)
-
-            @pl.loop(0, step, unroll=UNROLL)
-            def _(k):
+            for k, factors in enumerate(to_columns(factor)):
                 b = q * step + k
-                factors = column(k)
+                factors = cut(factors)
                 for s in range(SLOTS):
                     total = tree(jnp.add, [v * c for v, c in zip(strips(b, s), factors)])
-                    here = place_at(b * SLOTS + s)
-                    sums[here, :] = total * peaks[here, :]
+                    pair = place_at(s * sb + b)
+                    sums[pair, :] = total * peaks[pair, :]
 
         gam[pl.ds(0, tb), :] = sum_rows(
             it,
@@ -363,6 +376,9 @@
     dma = pltpu.SemaphoreType.DMA
     shared = (ITERS, n_rows, tb // n_rows, BLOCK)
     return [
+        pltpu.VMEM((sb, LIST), jnp.int32),
+        pltpu.VMEM((sb, BLOCK), jnp.int32),
+        pltpu.SMEM((sb, BLOCK), jnp.int32),
         pltpu.VMEM((dim, sb * BLOCK), bf16),
         pltpu.VMEM((tb + 1, dim, BLOCK), bf16),
         pltpu.VMEM((sb, BLOCK), f32),
@@ -376,16 +392,14 @@
         pltpu.VMEM((pairs, pairs), bf16),
         pltpu.VMEM((tb, pairs), bf16),
         pltpu.VMEM((tb, pairs), bf16),
-        pltpu.VMEM((BLOCK, sb // CHUNKS * BLOCK), bf16),
         pltpu.VMEM((len(SCAN), pairs, BLOCK), f32),
         pltpu.VMEM((pairs * SUB, BLOCK), f32),
         pltpu.VMEM((pairs * SUB, BLOCK), f32),
-        pltpu.VMEM((sb // CHUNKS, BLOCK, BLOCK), f32),
         pltpu.VMEM((ITERS, n_cols, sb, BLOCK), f32),
         pltpu.VMEM(shared, f32),
         pltpu.VMEM(shared, f32),
         pltpu.VMEM(shared, f32),
-        dma((3,)),
+        dma((5,)),
         dma((GROUPS,)),
         dma((ITERS,)),
         dma((ITERS, CHUNKS)),
@@ -405,12 +419,11 @@
             jax.ShapeDtypeStruct((sb, BLOCK), jnp.float32),
             jax.ShapeDtypeStruct((tb, BLOCK), jnp.float32),
         ),
-        in_specs=[pl.BlockSpec(memory_space=pltpu.SMEM), vmem, vmem]
-        + [pl.BlockSpec(memory_space=pl.ANY)] * 4,
+        in_specs=[pl.BlockSpec(memory_space=pltpu.HBM)] * 5,
         out_specs=(vmem, vmem),
         scratch_shapes=scratch(n_rows, n_cols, dim, sb, tb),
         compiler_params=pltpu.CompilerParams(
-            collective_id=0 if remote else None, has_side_effects=True, vmem_limit_bytes=48 * 2**20
+            collective_id=0 if remote else None, has_side_effects=True, vmem_limit_bytes=62 * 2**20
         ),
         cost_estimate=pl.CostEstimate(
             flops=2 * pairs * dim * BLOCK * BLOCK,
@@ -423,17 +436,9 @@
 def on_device(n_rows, n_cols, source_cells, target_cells, source_logmass, target_logmass, neighbours):
     sb = neighbours.shape[0]
     tb = target_cells.shape[1] // BLOCK
-    pairs = sb * SLOTS
-    local = neighbours - lax.axis_index("cols") * tb
-    owned = (local >= 0) & (local < tb)
-    upto = jnp.arange(LIST)[:, None] <= jnp.arange(LIST)[None, :]
-    nth = jnp.sum(jnp.where(owned[:, :, None] & upto[None], 1, 0), axis=1)
-    wanted = (nth[:, :, None] == 1 + jnp.arange(SLOTS)[None, None, :]) & owned[:, :, None]
-    ids = tb + jnp.sum(jnp.where(wanted, local[:, :, None] - tb, 0), axis=1)
-    ids = ids.reshape(pairs).astype(jnp.int32)
     f, g = make_call(n_rows, n_cols, source_cells.shape[0], sb, tb)(
-        ids, ids.reshape(1, pairs), ids.reshape(pairs, 1), source_cells, target_cells,
-        source_logmass.reshape(sb, BLOCK), target_logmass.reshape(tb, BLOCK),
+        source_cells, target_cells, source_logmass.reshape(sb, BLOCK),
+        target_logmass.reshape(tb, BLOCK), neighbours,
     )
     return f.reshape(-1), g.reshape(-1)
 

time: 94.9 us -> 84.5 us (0.89)
  Pallas kernels: 85.5 us -> 78.9 us
  local copies, waits for them, and re-layouts: 6.74 us -> 4.34 us
  other arithmetic: 1.63 us -> 0 us
    pallas_call x1, Pallas kernels: 85.5 us -> 78.9 us  [on_device(): make_call(n_rows, n_cols, source_cells.shape[0], sb, tb)]
    unnamed x10 -> x3, local copies, waits for them, and re-layouts: 6.35 us -> 4.34 us
where the time goes in v3:
time: 84.5 us; the launch traced here: 83.9 us
  Pallas kernels  78.9 us (93%)
  local copies, waits for them, and re-layouts  4.34 us (5%)
    pallas_call x1, Pallas kernels, on_device(): make_call(n_rows, n_cols, source_cells.shape[0], sb, tb)  78.9 us
    unnamed x3, local copies, waits for them, and re-layouts  4.34 us

profile of v3, /device:TPU:1, one launch (start us, length us, event | category | flops | bytes accessed | tf_op | source)
XLA Modules:
  0.0 83.9 jit_solution(18393039210285247378)
XLA Ops:
  0.6 1.4 %copy.7.n_hbm = s32[64,16]{1,0:T(8,128)} copy(s32[64,16]{0,1:T(8,128)} %param.9) | data formatting | bytes 8192 | tf_op args[4]
  2.0 78.9 %shard_map.68 = (f32[64,128]{1,0:T(8,128)}, f32[256,128]{1,0:T(8,128)}) custom-call(bf16[64,8192]{1,0:T(8,128)(2,1)} %x_hbm.1, bf16[64,32768]{1,0:T(8,128)(2,1)} %y_hbm.1, f32[64,128]{1,0:T(8,128)} %bitcast.7, f32[256,128]{1,0:T(8,128)} %bitcast.6, s32[64,16]{1,0:T(8,128)} %copy.7.n_hbm), custom_call_target="tpu_custom_call" | custom-call | flops 536870912 | bytes 5242880 | tf_op jit(solution)/shard_map/pallas_call | solution.py:439
  80.9 1.4 %copy.10 = f32[8192]{0:T(1024)} copy(f32[8192]{0:T(1024)} %bitcast.5) | data formatting | bytes 65536
  82.3 1.6 %copy.11 = f32[32768]{0:T(1024)} copy(f32[32768]{0:T(1024)} %bitcast.4) | data formatting | bytes 262144

commit v4 on v3

--- a/solution.py
+++ b/solution.py
@@ -18,6 +18,8 @@
 LOG2E = math.log2(math.e)
 UNIT = EPS / LOG2E
 CHUNKS = 4
+ROW_NEAR = 4
+COL_NEAR = 2
 GROUPS = 8
 SCAN = (1, 2, 4, 8, 16, 32)
 UNROLL = 16
@@ -41,6 +43,16 @@
     rest = v - high
     middle = rest.astype(jnp.bfloat16).astype(jnp.float32)
     return [high, middle, rest - middle]
+
+
+def swing(k, n):
+    return n // 2 + (k + 1) // 2 * (1 - 2 * (k % 2))
+
+
+def peer_of(k, me, n, near):
+    far = n // near
+    there = lax.rem(me // near + swing(k // near, far), far)
+    return there * near + lax.rem(lax.rem(me, near) + swing(lax.rem(k, near), near), near)
 
 
 def pick(onehot, v):
@@ -67,17 +79,20 @@
         me_r, me_c = lax.axis_index("rows"), lax.axis_index("cols")
         barrier = pltpu.get_barrier_semaphore()
 
-        @pl.loop(1, n_rows)
-        def _(d):
-            pl.semaphore_signal(
-                barrier, inc=1, device_id={"rows": lax.rem(me_r + d, n_rows)}, device_id_type=MESH
-            )
-
-        @pl.loop(1, n_cols)
-        def _(d):
-            pl.semaphore_signal(
-                barrier, inc=1, device_id={"cols": lax.rem(me_c + d, n_cols)}, device_id_type=MESH
-            )
+        def row_peer(k):
+            return {"rows": peer_of(k, me_r, n_rows, math.gcd(ROW_NEAR, n_rows))}
+
+        def col_peer(k):
+            return {"cols": peer_of(k, me_c, n_cols, math.gcd(COL_NEAR, n_cols))}
+
+        @pl.loop(0, n_rows - 1)
+        def _(k):
+            pl.semaphore_signal(barrier, inc=1, device_id=row_peer(k), device_id_type=MESH)
+
+        @pl.loop(0, n_cols - 1)
+        def _(k):
+            pl.semaphore_signal(barrier, inc=1, device_id=col_peer(k), device_id_type=MESH)
+
     else:
         me_r = me_c = 0
 
@@ -108,25 +123,25 @@
     ik = lax.broadcasted_iota(jnp.int32, (LIST, LIST), 0)
     il = lax.broadcasted_iota(jnp.int32, (LIST, LIST), 1)
     nth = jnp.dot(
+        jnp.where(il <= ik, 1.0, 0.0).astype(jnp.bfloat16),
         jnp.where(owned, 1.0, 0.0).astype(jnp.bfloat16),
-        jnp.where(ik <= il, 1.0, 0.0).astype(jnp.bfloat16),
         preferred_element_type=jnp.float32,
     )
     away = local.astype(jnp.float32) - tb
     slots = [
-        jnp.sum(jnp.where(owned & (nth == s + 1.0), away, 0.0), axis=1, keepdims=True) + tb
+        jnp.sum(jnp.where(owned & (nth == s + 1.0), away, 0.0), axis=0, keepdims=True) + tb
         for s in range(SLOTS)
     ]
-    at_lane = lax.broadcasted_iota(jnp.int32, (sb, BLOCK), 1)
-    ids = sum(jnp.where(at_lane == s, slots[s], 0.0) for s in range(SLOTS)).astype(jnp.int32)
-    listed[...] = jnp.minimum(jnp.maximum(ids, 0), tb)
+    ids = jnp.concatenate(slots + [jnp.zeros((SUB - SLOTS, sb), jnp.float32)], axis=0)
+    ids = jnp.concatenate([ids, jnp.zeros((SUB, BLOCK - sb), jnp.float32)], axis=1)
+    listed[...] = jnp.minimum(jnp.maximum(ids.astype(jnp.int32), 0), tb)
     to_scalars = pltpu.make_async_copy(listed, ids_ref, x_sem.at[4])
     to_scalars.start()
 
-    tc = jnp.concatenate(slots, axis=0)
+    tr = jnp.concatenate(slots, axis=1)
     ip = lax.broadcasted_iota(jnp.int32, (pairs, pairs), 0)
     iq = lax.broadcasted_iota(jnp.int32, (pairs, pairs), 1)
-    tr = jnp.sum(jnp.where(ip == iq, tc, 0.0), axis=0, keepdims=True)
+    tc = jnp.sum(jnp.where(ip == iq, tr, 0.0), axis=1, keepdims=True)
     before = (tc < tr) | ((tc == tr) & (ip < iq))
     place = jnp.sum(jnp.where(before, 1.0, 0.0), axis=0, keepdims=True)
     put = place == ip.astype(jnp.float32)
@@ -163,24 +178,19 @@
     for copy in fetch:
         copy.wait()
 
-    @pl.loop(0, sb, unroll=UNROLL)
-    def _(b):
-        cells = x_ref[:, pl.ds(pl.multiple_of(b * BLOCK, BLOCK), BLOCK)].astype(jnp.float32)
-        sqx[pl.ds(b, 1), :] = jnp.sum(cells * cells, axis=0, keepdims=True) * (0.5 * kappa)
-
     def chunk(q):
         return pl.ds(pl.multiple_of(q * step, step), step)
 
     def send_rows(it, q):
         if remote:
 
-            @pl.loop(1, n_cols)
-            def _(d):
+            @pl.loop(0, n_cols - 1)
+            def _(k):
                 there = src.at[it, me_c, chunk(q)]
                 pltpu.make_async_remote_copy(
                     src_ref=there, dst_ref=there,
                     send_sem=src_send.at[it], recv_sem=src_recv.at[it, q],
-                    device_id={"cols": lax.rem(me_c + d, n_cols)}, device_id_type=MESH,
+                    device_id=col_peer(k), device_id_type=MESH,
                 ).start()
 
     def rows_landed(it, q):
@@ -193,19 +203,27 @@
         tall = jnp.concatenate([v, jnp.zeros((BLOCK - step, BLOCK), jnp.float32)], axis=0).T
         return [jnp.broadcast_to(tall[:, k : k + 1], (BLOCK, BLOCK)) for k in range(step)]
 
+    def source_squares():
+        @pl.loop(0, sb, unroll=UNROLL)
+        def _(b):
+            cells = x_ref[:, pl.ds(pl.multiple_of(b * BLOCK, BLOCK), BLOCK)].astype(jnp.float32)
+            sqx[pl.ds(b, 1), :] = jnp.sum(cells * cells, axis=0, keepdims=True) * (0.5 * kappa)
+
     def sum_rows(it, v, combine):
         trg[it] = v.reshape(n_rows, share, BLOCK)
         if remote:
 
-            @pl.loop(1, n_rows)
-            def _(d):
-                peer = lax.rem(me_r + d, n_rows)
+            @pl.loop(0, n_rows - 1)
+            def _(k):
+                peer = row_peer(k)
                 pltpu.make_async_remote_copy(
-                    src_ref=trg.at[it, peer], dst_ref=landing.at[it, me_r],
+                    src_ref=trg.at[it, peer["rows"]], dst_ref=landing.at[it, me_r],
                     send_sem=trg_send.at[it], recv_sem=trg_recv.at[it],
-                    device_id={"rows": peer}, device_id_type=MESH,
+                    device_id=peer, device_id_type=MESH,
                 ).start()
 
+        if it == 0:
+            source_squares()
         landing[it, me_r] = trg[it, me_r]
         if remote:
             landed = landing.at[it, pl.ds(0, n_rows - 1)]
@@ -213,12 +231,12 @@
         own[it, me_r] = combine(landing[it])
         if remote:
 
-            @pl.loop(1, n_rows)
-            def _(d):
+            @pl.loop(0, n_rows - 1)
+            def _(k):
                 pltpu.make_async_remote_copy(
                     src_ref=own.at[it, me_r], dst_ref=own.at[it, me_r],
                     send_sem=own_send.at[it], recv_sem=own_recv.at[it],
-                    device_id={"rows": lax.rem(me_r + d, n_rows)}, device_id_type=MESH,
+                    device_id=row_peer(k), device_id_type=MESH,
                 ).start()
 
             landed = own.at[it, pl.ds(0, n_rows - 1)]
@@ -245,7 +263,7 @@
         def _(k):
             b = q * step + k
             cells = x_ref[:, pl.ds(pl.multiple_of(b * BLOCK, BLOCK), BLOCK)]
-            ids = [ids_ref[b, s] for s in range(SLOTS)]
+            ids = [ids_ref[s, b] for s in range(SLOTS)]
             crossed = lax.dot_general(
                 cells, jnp.concatenate([cells_y[t] for t in ids], axis=1), (((0,), (0,)), ((), ())),
                 preferred_element_type=jnp.float32,
@@ -320,7 +338,7 @@
                 weights = []
                 for s in range(SLOTS):
                     here = place_at(s * sb + b)
-                    row = gam[ids_ref[b, s]][None, :]
+                    row = gam[ids_ref[s, b]][None, :]
                     if it == 1:
                         peaks[here, :] = jnp.exp2(peaks[here, :] + row)
                         weights.append(peaks[here, :])
@@ -376,9 +394,9 @@
     dma = pltpu.SemaphoreType.DMA
     shared = (ITERS, n_rows, tb // n_rows, BLOCK)
     return [
-        pltpu.VMEM((sb, LIST), jnp.int32),
-        pltpu.VMEM((sb, BLOCK), jnp.int32),
-        pltpu.SMEM((sb, BLOCK), jnp.int32),
+        pltpu.VMEM((LIST, sb), jnp.int32),
+        pltpu.VMEM((SUB, BLOCK), jnp.int32),
+        pltpu.SMEM((SUB, BLOCK), jnp.int32),
         pltpu.VMEM((dim, sb * BLOCK), bf16),
         pltpu.VMEM((tb + 1, dim, BLOCK), bf16),
         pltpu.VMEM((sb, BLOCK), f32),
@@ -416,14 +434,14 @@
     return pl.pallas_call(
         functools.partial(kernel, n_rows, n_cols, remote),
         out_shape=(
-            jax.ShapeDtypeStruct((sb, BLOCK), jnp.float32),
-            jax.ShapeDtypeStruct((tb, BLOCK), jnp.float32),
+            pltpu.VMEM((sb, BLOCK), jnp.float32),
+            pltpu.VMEM((tb, BLOCK), jnp.float32),
         ),
         in_specs=[pl.BlockSpec(memory_space=pltpu.HBM)] * 5,
         out_specs=(vmem, vmem),
         scratch_shapes=scratch(n_rows, n_cols, dim, sb, tb),
         compiler_params=pltpu.CompilerParams(
-            collective_id=0 if remote else None, has_side_effects=True, vmem_limit_bytes=62 * 2**20
+            collective_id=0 if remote else None, has_side_effects=True, vmem_limit_bytes=60 * 2**20
         ),
         cost_estimate=pl.CostEstimate(
             flops=2 * pairs * dim * BLOCK * BLOCK,
@@ -438,7 +456,7 @@
     tb = target_cells.shape[1] // BLOCK
     f, g = make_call(n_rows, n_cols, source_cells.shape[0], sb, tb)(
         source_cells, target_cells, source_logmass.reshape(sb, BLOCK),
-        target_logmass.reshape(tb, BLOCK), neighbours,
+        target_logmass.reshape(tb, BLOCK), neighbours.T,
     )
     return f.reshape(-1), g.reshape(-1)
 

time: 84.5 us -> 75.7 us (0.90)
  Pallas kernels: 78.9 us -> 73.7 us
  local copies, waits for them, and re-layouts: 4.34 us -> 1.28 us
    pallas_call x1, Pallas kernels: 78.9 us -> 73.7 us  [on_device(): make_call(n_rows, n_cols, source_cells.shape[0], sb, tb)]
    unnamed x3 -> x2, local copies, waits for them, and re-layouts: 4.34 us -> 1.28 us
where the time goes in v4:
time: 75.7 us; the launch traced here: 75.6 us
  Pallas kernels  73.7 us (97%)
  local copies, waits for them, and re-layouts  1.28 us (2%)
    pallas_call x1, Pallas kernels, on_device(): make_call(n_rows, n_cols, source_cells.shape[0], sb, tb)  73.7 us

profile of v4, /device:TPU:1, one launch (start us, length us, event | category | flops | bytes accessed | tf_op | source)
XLA Modules:
  0.0 75.6 jit_solution(797983625097189948)
XLA Ops:
  0.6 73.7 %shard_map.68 = (f32[64,128]{1,0:T(8,128)S(1)}, f32[256,128]{1,0:T(8,128)S(1)}) custom-call(bf16[64,8192]{1,0:T(8,128)(2,1)} %x_hbm.1, bf16[64,32768]{1,0:T(8,128)(2,1)} %y_hbm.1, f32[64,128]{1,0:T(8,128)} %bitcast.8, f32[256,128]{1,0:T(8,128)} %bitcast.7, s32[16,64]{1,0:T(8,128)} %bitcast.9), custom_call_target="tpu_custom_call" | custom-call | flops 536870912 | bytes 5242880 | tf_op jit(solution)/shard_map/pallas_call | solution.py:457
  74.3 0.6 copy.9
  74.9 0.7 copy.10

commit v5 on v4

--- a/solution.py
+++ b/solution.py
@@ -52,7 +52,7 @@
 def peer_of(k, me, n, near):
     far = n // near
     there = lax.rem(me // near + swing(k // near, far), far)
-    return there * near + lax.rem(lax.rem(me, near) + swing(lax.rem(k, near), near), near)
+    return there * near + lax.rem(lax.rem(me, near) + swing(k % near, near), near)
 
 
 def pick(onehot, v):
@@ -184,8 +184,7 @@
     def send_rows(it, q):
         if remote:
 
-            @pl.loop(0, n_cols - 1)
-            def _(k):
+            for k in range(n_cols - 1):
                 there = src.at[it, me_c, chunk(q)]
                 pltpu.make_async_remote_copy(
                     src_ref=there, dst_ref=there,
@@ -213,8 +212,7 @@
         trg[it] = v.reshape(n_rows, share, BLOCK)
         if remote:
 
-            @pl.loop(0, n_rows - 1)
-            def _(k):
+            for k in range(n_rows - 1):
                 peer = row_peer(k)
                 pltpu.make_async_remote_copy(
                     src_ref=trg.at[it, peer["rows"]], dst_ref=landing.at[it, me_r],
@@ -231,8 +229,7 @@
         own[it, me_r] = combine(landing[it])
         if remote:
 
-            @pl.loop(0, n_rows - 1)
-            def _(k):
+            for k in range(n_rows - 1):
                 pltpu.make_async_remote_copy(
                     src_ref=own.at[it, me_r], dst_ref=own.at[it, me_r],
                     send_sem=own_send.at[it], recv_sem=own_recv.at[it],

time: 75.7 us -> 74 us (0.978)
  Pallas kernels: 73.7 us -> 72 us
    pallas_call x1, Pallas kernels: 73.7 us -> 72 us  [on_device(): make_call(n_rows, n_cols, source_cells.shape[0], sb, tb)]
where the time goes in v5:
time: 74 us; the launch traced here: 73.9 us
  Pallas kernels  72 us (97%)
  local copies, waits for them, and re-layouts  1.28 us (2%)
    pallas_call x1, Pallas kernels, on_device(): make_call(n_rows, n_cols, source_cells.shape[0], sb, tb)  72 us

profile of v5, /device:TPU:1, one launch (start us, length us, event | category | flops | bytes accessed | tf_op | source)
XLA Modules:
  0.0 73.9 jit_solution(8854095843033203261)
XLA Ops:
  0.6 72.0 %shard_map.68 = (f32[64,128]{1,0:T(8,128)S(1)}, f32[256,128]{1,0:T(8,128)S(1)}) custom-call(bf16[64,8192]{1,0:T(8,128)(2,1)} %x_hbm.1, bf16[64,32768]{1,0:T(8,128)(2,1)} %y_hbm.1, f32[64,128]{1,0:T(8,128)} %bitcast.8, f32[256,128]{1,0:T(8,128)} %bitcast.7, s32[16,64]{1,0:T(8,128)} %bitcast.9), custom_call_target="tpu_custom_call" | custom-call | flops 536870912 | bytes 5242880 | tf_op jit(solution)/shard_map/pallas_call | solution.py:454
  72.6 0.6 copy.9
  73.3 0.7 copy.10

commit v6 on v5

--- a/solution.py
+++ b/solution.py
@@ -51,6 +51,12 @@
 
 def peer_of(k, me, n, near):
     far = n // near
+    if isinstance(k, int):
+        away = [(i, j) for i in range(far) for j in range(near) if i or j]
+        away.sort(key=lambda o: -min(o[0], far - o[0]) - min(o[1], near - o[1]))
+        i, j = away[k]
+        there = lax.rem(me // near + i, far)
+        return there * near + lax.rem(lax.rem(me, near) + j, near)
     there = lax.rem(me // near + swing(k // near, far), far)
     return there * near + lax.rem(lax.rem(me, near) + swing(k % near, near), near)
 

time: 74 us -> 73.5 us (level)
  Pallas kernels: 72 us -> 71.2 us
    pallas_call x1, Pallas kernels: 72 us -> 71.2 us  [on_device(): make_call(n_rows, n_cols, source_cells.shape[0], sb, tb)]
where the time goes in v6:
time: 73.5 us; the launch traced here: 73.1 us
  Pallas kernels  71.2 us (97%)
  local copies, waits for them, and re-layouts  1.28 us (2%)
    pallas_call x1, Pallas kernels, on_device(): make_call(n_rows, n_cols, source_cells.shape[0], sb, tb)  71.2 us

profile of v6, /device:TPU:1, one launch (start us, length us, event | category | flops | bytes accessed | tf_op | source)
XLA Modules:
  0.0 73.1 jit_solution(17924682599287009804)
XLA Ops:
  0.6 71.2 %shard_map.68 = (f32[64,128]{1,0:T(8,128)S(1)}, f32[256,128]{1,0:T(8,128)S(1)}) custom-call(bf16[64,8192]{1,0:T(8,128)(2,1)} %x_hbm.1, bf16[64,32768]{1,0:T(8,128)(2,1)} %y_hbm.1, f32[64,128]{1,0:T(8,128)} %bitcast.8, f32[256,128]{1,0:T(8,128)} %bitcast.7, s32[16,64]{1,0:T(8,128)} %bitcast.9), custom_call_target="tpu_custom_call" | custom-call | flops 536870912 | bytes 5242880 | tf_op jit(solution)/shard_map/pallas_call | solution.py:460
  71.8 0.6 copy.9
  72.4 0.7 copy.10
